TPU v7x, 32 devices: a whole 2x2x4 slice. The times are simulated.
32 devices in a mesh: group: 2 (over x), span: 16 (over z, y, core).
Axes of the slice: x: 2, y: 2, z: 4, core: 2. Of those that a mesh axis runs over, the one named last changes fastest.
Arguments:
- queries: bfloat16 [8192, 2560], P(('group', 'span')), parts along dimension 0, may hold values from -6 to 6
- keys_values: bfloat16 [2, 8192, 2560], P(None, ('group', 'span')), parts along dimension 1, may hold values from -6 to 6
- owner: int32 [2], P('group'), parts along dimension 0, may hold values from 0 to 15
- span_mask: int32 [32, 3], P('group'), parts along dimension 0, may hold values 0 or 1
- lengths: int32 [32], P('group'), parts along dimension 0, may hold values from 128 to 256, as said below
- frames: bfloat16 [6, 16, 52, 384], P('group', 'span'), parts along dimension 0, may hold values from -6 to 6
- past_frames: bfloat16 [4, 16, 52, 384], P('group', 'span'), parts along dimension 0, may hold values from -5 to 5
- norm_gain: float32 [384], replicated, may hold values from 0.5 to 1.5
- conv_weight: bfloat16 [3, 3, 3, 384, 384], replicated, may hold values from -0.0625 to 0.0625
- conv_bias: float32 [384], replicated, may hold values from -3 to 3
Outputs:
- attended: bfloat16 [8192, 2560], P(('group', 'span')), parts along dimension 0
- decoded: bfloat16 [6, 16, 52, 384], P('group', 'span'), parts along dimension 0
There are 2 independent parts, one for each index of `group`. A program takes and returns all parts, laid end to end along the dimension named above; an argument that names none is the same for every part. Nothing has to cross between parts.
Inputs may be any that keep to these rules, and one draw needn't show every extreme that they name: `lengths`: at least one slot holds exactly 256 tokens.
All inputs are finite; a program needn't handle non-finite values.
Results may differ from a plain program's by a relative error of at most 0.005.
Values may be sent and summed in bfloat16 or wider, within the bound.
A program may use at most 128 MiB of HBM per device.

v0:
```python
import jax
import jax.numpy as jnp
from jax import lax
from jax.sharding import PartitionSpec as P

H = 20
DH = 128
WIN = 4


def from_behind(value, axis, steps):
    count = lax.axis_size(axis)
    pairs = [(source, (source + steps) % count) for source in range(count)]
    return lax.ppermute(value, axis, pairs)


def spread(block, axis, source):
    block = jnp.where(lax.axis_index(axis) == source, block, jnp.zeros_like(block))
    return lax.psum(block, axis)


def extended_2(block, sides, width):
    for axis, dim in sides:
        count = lax.axis_size(axis)
        forward = [(i, i + 1) for i in range(count - 1)]
        backward = [(target, source) for source, target in forward]
        low = lax.ppermute(
            lax.slice_in_dim(block, block.shape[dim] - width, None, axis=dim), axis, forward
        )
        high = lax.ppermute(lax.slice_in_dim(block, 0, width, axis=dim), axis, backward)
        block = jnp.concatenate([low, block, high], axis=dim)
    return block


def shards(
    queries,
    keys_values,
    owner,
    span_mask,
    lengths,
    frames,
    past_frames,
    norm_gain,
    conv_weight,
    conv_bias,
):
    devices = lax.axis_size("span")
    place = lax.axis_index("span")
    anchor = owner[0]
    position = (place - anchor - 1) % devices
    tok_rows = queries.shape[0]
    row_ids = jnp.arange(tok_rows, dtype=jnp.int32)
    blocks = [keys_values]
    valid_list = [row_ids < lengths[place]]
    for offset in range(1, WIN):
        blocks.append(from_behind(keys_values, "span", offset))
    for offset in range(1, WIN):
        source = (place - offset) % devices
        allowed = (position >= offset) & (span_mask[position, offset - 1] == 1)
        valid_list.append(allowed & (row_ids < lengths[source]))
    blocks.append(spread(keys_values, "span", anchor))
    valid_list.append((place != anchor) & (row_ids < lengths[anchor]))
    gathered = jnp.concatenate(blocks, axis=1)
    key_valid = jnp.concatenate(valid_list)
    score_scale = DH ** (-0.5)
    pieces = []
    for head_block in range(H // 4):
        first_col = head_block * 4 * DH
        last_col = first_col + 4 * DH
        query_group = queries[:, first_col:last_col].reshape(tok_rows, 4, DH)
        key_group = gathered[0, :, first_col:last_col].reshape(-1, 4, DH)
        value_group = gathered[1, :, first_col:last_col].reshape(-1, 4, DH)
        scores = (
            jnp.einsum("qhd,khd->hqk", query_group, key_group, preferred_element_type=jnp.float32)
            * score_scale
        )
        scores = jnp.where(key_valid[None, None, :], scores, -jnp.inf)
        row_max = jnp.max(scores, axis=-1, keepdims=True)
        weights = jnp.exp(scores - row_max)
        probs = (weights / jnp.sum(weights, axis=-1, keepdims=True)).astype(jnp.bfloat16)
        blended = jnp.einsum("hqk,khd->qhd", probs, value_group, preferred_element_type=jnp.float32)
        pieces.append(blended.reshape(tok_rows, 4 * DH))
    attended = jnp.concatenate(pieces, axis=1)
    attended = jnp.where(row_ids[:, None] < lengths[place], attended, 0.0).astype(jnp.bfloat16)
    features = frames.astype(jnp.float32)
    squares = jnp.mean(features * features, axis=-1, keepdims=True)
    normed = features * lax.rsqrt(squares + 1e-06) * norm_gain
    activated = jax.nn.silu(normed).astype(jnp.bfloat16)
    stacked = jnp.concatenate([past_frames, activated], axis=0)
    extended = extended_2(stacked, (("span", 1),), 1)
    padded = jnp.pad(extended, ((0, 0), (0, 0), (1, 1), (0, 0)))
    frame_count = frames.shape[0]
    rows_here = frames.shape[1]
    col_count = frames.shape[2]
    channels = frames.shape[3]
    windows = []
    for frame_tap in range(3):
        for row_tap in range(3):
            for col_tap in range(3):
                windows.append(
                    padded[
                        frame_tap : frame_tap + frame_count,
                        row_tap : row_tap + rows_here,
                        col_tap : col_tap + col_count,
                        :,
                    ]
                )
    columns = jnp.concatenate(windows, axis=-1).reshape(-1, 27 * channels)
    convolved = jnp.dot(
        columns, conv_weight.reshape(27 * channels, channels), preferred_element_type=jnp.float32
    )
    decoded = features + conv_bias + convolved.reshape(frame_count, rows_here, col_count, channels)
    return (attended, decoded.astype(jnp.bfloat16))


def solution(mesh):
    placed = (
        P(("group", "span"), None),
        P(None, ("group", "span"), None),
        P("group"),
        P("group", None),
        P("group"),
        P("group", "span", None, None),
        P("group", "span", None, None),
        P(),
        P(),
        P(),
    )
    return jax.shard_map(
        shards,
        mesh=mesh,
        in_specs=placed,
        out_specs=(P(("group", "span"), None), P("group", "span", None, None)),
        check_vma=False,
    )
```

profile of v0, /device:TPU:0, one launch (start us, length us, event | category | flops | bytes accessed | tf_op | source)
XLA Modules:
  0.0 295.0 jit_solution(9412599492333403696)
XLA Ops:
  7.2 3.0 %copy.34 = bf16[2,256,2560]{1,2,0:T(8,128)(2,1)S(1)} copy(bf16[2,256,2560]{2,1,0:T(8,128)(2,1)} %param.11) | data formatting | bytes 5242880 | tf_op args[1]
  10.8 2.6 collective-permute-start.1
  13.3 2.4 collective-permute-start.2
  18.1 3.0 %collective-permute-start.3 = (bf16[5,1,52,384]{3,2,0,1:T(8,128)(2,1)}, bf16[5,1,52,384]{3,2,0,1:T(8,128)(2,1)S(1)}, u32[]{:S(2)}, u32[]{:S(2)}) collective-permute-start(bf16[5,1,52,384]{3,2,0,1:T(8,128)(2,1)} %pad_maximum_fusion), channel_id=1, source_target_pairs={{0,1},{1,2},{2,3},{3,4},{4,5},{5,6},{6,7},{7,8},{8,9},{9,10},{10,1... | collective-permute-start | bytes 599048 | tf_op jit(solution)/shard_map/ppermute | solution.py:27
  21.8 3.3 %broadcast_select_fusion = (bf16[2,256,2560]{1,2,0:T(8,128)(2,1)}, bf16[2,1280,2560]{1,2,0:T(8,128)(2,1)}) fusion(bf16[2,256,2560]{1,2,0:T(8,128)(2,1)S(1)} %copy.34, pred[]{:T(512)S(6)} %eq.26), kind=kLoop, calls=%fused_computation.38 | loop fusion | flops 1310719 | bytes 7864321 | tf_op jit(solution)/shard_map/jit(_where)/select_n | solution.py:18
  25.2 2.4 fusion.101
  27.6 1.8 copy.78
  33.1 1.8 copy.79
  34.9 1.8 copy.80
  36.7 1.8 copy.81
  38.5 1.8 copy.82
  45.0 6.0 %fusion.32 = bf16[3,1,52,384]{3,2,1,0:T(8,128)(2,1)} fusion(bf16[10368,384,1]{1,0,2:T(8,128)(2,1)} %bitcast.151, bf16[3,1,52,10368]{3,2,0,1:T(8,128)(2,1)S(1)} %slice_dynamic-update-slice_fusion, bf16[3,1,52,384]{3,2,1,0:T(8,128)(2,1)S(1)} %copy-done, f32[384]{0:T(512)S(1)} %copy-done.8), kind=kOutput, calls=%fused_computation.50 | convolution fusion | flops 1242408960 | bytes 11438592 | tf_op jit(solution)/shard_map/dot_general | solution.py:109
  51.0 41.6 %collective-permute-done = bf16[2,256,2560]{1,2,0:T(8,128)(2,1)} collective-permute-done((bf16[2,256,2560]{1,2,0:T(8,128)(2,1)S(1)}, bf16[2,256,2560]{1,2,0:T(8,128)(2,1)}, u32[]{:S(2)}, u32[]{:S(2)}) %collective-permute-start) | collective-permute-done | bytes 2621472 | tf_op jit(solution)/shard_map/ppermute | solution.py:14
  92.6 3.5 %constant_dynamic-update-slice_fusion.3 = bf16[2,1280,2560]{1,2,0:T(8,128)(2,1)} fusion(bf16[2,1280,2560]{1,2,0:T(8,128)(2,1)} %get-tuple-element.17, bf16[2,256,2560]{1,2,0:T(8,128)(2,1)} %collective-permute-done), kind=kLoop, calls=%fused_computation.103 | loop fusion | bytes 5242880
  96.2 3.6 %constant_dynamic-update-slice_fusion.2 = bf16[2,1280,2560]{1,2,0:T(8,128)(2,1)} fusion(bf16[2,1280,2560]{1,2,0:T(8,128)(2,1)} %constant_dynamic-update-slice_fusion.3, bf16[2,256,2560]{1,2,0:T(8,128)(2,1)} %collective-permute-done.1), kind=kLoop, calls=%fused_computation.102 | loop fusion | bytes 5242880
  99.8 38.6 %collective-permute-done.2 = bf16[2,256,2560]{1,2,0:T(8,128)(2,1)} collective-permute-done((bf16[2,256,2560]{1,2,0:T(8,128)(2,1)S(1)}, bf16[2,256,2560]{1,2,0:T(8,128)(2,1)}, u32[]{:S(2)}, u32[]{:S(2)}) %collective-permute-start.2) | collective-permute-done | bytes 2621472 | tf_op jit(solution)/shard_map/ppermute | solution.py:14
  138.4 3.5 %constant_dynamic-update-slice_fusion.1 = bf16[2,1280,2560]{1,2,0:T(8,128)(2,1)} fusion(bf16[2,1280,2560]{1,2,0:T(8,128)(2,1)} %constant_dynamic-update-slice_fusion.2, bf16[2,256,2560]{1,2,0:T(8,128)(2,1)} %collective-permute-done.2), kind=kLoop, calls=%fused_computation.101 | loop fusion | bytes 5242880
  141.8 86.6 %all-reduce.3.cloned.1.call-done = bf16[2,256,2560]{1,2,0:T(8,128)(2,1)} async-done(((bf16[2,256,2560]{1,2,0:T(8,128)(2,1)}), bf16[2,256,2560]{1,2,0:T(8,128)(2,1)}) %all-reduce.3.cloned.1.call-update) | async-done | bytes 2621456 | tf_op jit(solution)/shard_map/psum | solution.py:19
  228.4 3.5 %constant_dynamic-update-slice_fusion = bf16[2,1280,2560]{1,2,0:T(8,128)(2,1)} fusion(bf16[2,1280,2560]{1,2,0:T(8,128)(2,1)} %constant_dynamic-update-slice_fusion.1, bf16[2,256,2560]{1,2,0:T(8,128)(2,1)} %all-reduce.3.cloned.1.call-done), kind=kLoop, calls=%fused_computation.100 | loop fusion | bytes 5242880 | tf_op jit(solution)/shard_map/concatenate | solution.py:63
  231.9 9.1 %fusion.100 = (bf16[1,1280,512]{1,2,0:T(8,128)(2,1)S(1)}, bf16[1,1280,512]{1,2,0:T(8,128)(2,1)}, bf16[1,1280,512]{1,2,0:T(8,128)(2,1)}, bf16[1,1280,512]{1,2,0:T...) fusion(bf16[2,1280,2560]{1,2,0:T(8,128)(2,1)} %constant_dynamic, ...), kind=kLoop, calls=%fused_computation.140 | loop fusion | bytes 26214400 | tf_op jit(solution)/shard_map/slice | solution.py:71
  241.0 2.0 exponential_reduce_fusion.4
  243.0 4.5 %fusion.17 = bf16[4,128,256]{2,1,0:T(8,128)(2,1)} fusion(bf16[1280,4,128]{0,2,1:T(8,128)(2,1)} %bitcast.166, f32[4,256]{1,0:T(4,128)S(1)} %exponential_reduce_fusion.4, bf16[1280,4,128]{0,2,1:T(8,128)(2,1)S(1)} %bitcast.165, bf16[256,4,128]{0,2,1:T(8,128)(2,1)S(1)} %bitcast.168, pred[1280]{0:T(1024)(128)(4,1)S(1)} %constant_dynamic-update-slice_fusion.11), kind=kOutput, calls=%fused_computation.39 | convolution fusion | flops 677644544 | bytes 3151104 | tf_op jit(solution)/shard_map/hqk,khd->qhd/dot_general | solution.py:81
  248.6 3.3 %exponential_reduce_fusion.3 = f32[4,256]{1,0:T(4,128)S(1)} fusion(bf16[1280,4,128]{0,2,1:T(8,128)(2,1)} %bitcast.161, bf16[256,4,128]{0,2,1:T(8,128)(2,1)S(1)} %bitcast.175, pred[1280]{0:T(1024)(128)(4,1)S(1)} %constant_dynamic-update-slice_fusion.11), kind=kOutput, calls=%fused_computation.33 | convolution fusion | flops 340788480 | bytes 1578240 | tf_op jit(solution)/shard_map/sub | solution.py:79
  252.0 4.8 %fusion.18 = bf16[4,128,256]{2,1,0:T(8,128)(2,1)} fusion(bf16[1280,4,128]{0,2,1:T(8,128)(2,1)} %bitcast.163, f32[4,256]{1,0:T(4,128)S(1)} %exponential_reduce_fusion.3, bf16[1280,4,128]{0,2,1:T(8,128)(2,1)} %bitcast.162, bf16[256,4,128]{0,2,1:T(8,128)(2,1)S(1)} %bitcast.176, pred[1280]{0:T(1024)(128)(4,1)S(1)} %constant_dynamic-update-slice_fusion.11), kind=kOutput, calls=%fused_computation.40 | convolution fusion | flops 677644544 | bytes 3151104 | tf_op jit(solution)/shard_map/hqk,khd->qhd/dot_general | solution.py:81
  257.9 3.3 %exponential_reduce_fusion.2 = f32[4,256]{1,0:T(4,128)S(1)} fusion(bf16[1280,4,128]{0,2,1:T(8,128)(2,1)} %bitcast.158, bf16[256,4,128]{0,2,1:T(8,128)(2,1)S(1)} %bitcast.173, pred[1280]{0:T(1024)(128)(4,1)S(1)} %constant_dynamic-update-slice_fusion.11), kind=kOutput, calls=%fused_computation.32 | convolution fusion | flops 340788480 | bytes 1578240 | tf_op jit(solution)/shard_map/sub | solution.py:79
  261.2 5.0 %fusion.19 = bf16[4,128,256]{2,1,0:T(8,128)(2,1)} fusion(bf16[1280,4,128]{0,2,1:T(8,128)(2,1)} %bitcast.160, f32[4,256]{1,0:T(4,128)S(1)} %exponential_reduce_fusion.2, bf16[1280,4,128]{0,2,1:T(8,128)(2,1)} %bitcast.159, bf16[256,4,128]{0,2,1:T(8,128)(2,1)S(1)} %bitcast.174, pred[1280]{0:T(1024)(128)(4,1)S(1)} %constant_dynamic-update-slice_fusion.11), kind=kOutput, calls=%fused_computation.41 | convolution fusion | flops 677644544 | bytes 3151104 | tf_op jit(solution)/shard_map/hqk,khd->qhd/dot_general | solution.py:81
  267.3 3.3 %exponential_reduce_fusion.1 = f32[4,256]{1,0:T(4,128)S(1)} fusion(bf16[1280,4,128]{0,2,1:T(8,128)(2,1)} %bitcast.155, bf16[256,4,128]{0,2,1:T(8,128)(2,1)} %bitcast.171, pred[1280]{0:T(1024)(128)(4,1)S(1)} %constant_dynamic-update-slice_fusion.11), kind=kOutput, calls=%fused_computation.31 | convolution fusion | flops 340788480 | bytes 1578240 | tf_op jit(solution)/shard_map/sub | solution.py:79
  270.7 4.9 %fusion.20 = bf16[4,128,256]{2,1,0:T(8,128)(2,1)} fusion(bf16[1280,4,128]{0,2,1:T(8,128)(2,1)} %bitcast.157, f32[4,256]{1,0:T(4,128)S(1)} %exponential_reduce_fusion.1, bf16[1280,4,128]{0,2,1:T(8,128)(2,1)} %bitcast.156, bf16[256,4,128]{0,2,1:T(8,128)(2,1)} %bitcast.172, pred[1280]{0:T(1024)(128)(4,1)S(1)} %constant_dynamic-update-slice_fusion.11), kind=kOutput, calls=%fused_computation.42 | convolution fusion | flops 677644544 | bytes 3151104 | tf_op jit(solution)/shard_map/hqk,khd->qhd/dot_general | solution.py:81
  275.5 1.8 copy.58
  277.3 2.9 exponential_reduce_fusion
  280.2 4.5 %fusion.21 = bf16[4,128,256]{2,1,0:T(8,128)(2,1)} fusion(bf16[1280,4,128]{0,2,1:T(8,128)(2,1)} %bitcast.154, f32[4,256]{1,0:T(4,128)S(1)} %exponential_reduce_fusion, bf16[1280,4,128]{0,2,1:T(8,128)(2,1)S(1)} %bitcast.153, bf16[256,4,128]{0,2,1:T(8,128)(2,1)} %bitcast.170, pred[1280]{0:T(1024)(128)(4,1)S(1)} %constant_dynamic-update-slice_fusion.11), kind=kOutput, calls=%fused_computation.43 | convolution fusion | flops 677644544 | bytes 3151104 | tf_op jit(solution)/shard_map/hqk,khd->qhd/dot_general | solution.py:81
  286.8 1.3 select_convert_fusion
  (81 shorter events, 14.7 us)
Async XLA Ops:
  7.2 8.6 %copy-start.5 = (bf16[2,1,52,384]{3,0,2,1:T(2,128)(2,1)S(1)}, bf16[2,1,52,384]{3,0,2,1:T(2,128)(2,1)}, u32[]{:S(2)}) copy-start(bf16[2,1,52,384]{3,0,2,1:T(2,128)(2,1)} %param.16) | copy-start | bytes 239620
  7.2 8.6 %copy-start = (bf16[3,1,52,384]{3,2,1,0:T(8,128)(2,1)S(1)}, bf16[3,1,52,384]{3,2,1,0:T(8,128)(2,1)}, u32[]{:S(2)}) copy-start(bf16[3,1,52,384]{3,2,1,0:T(8,128)(2,1)} %param.15) | copy-start | bytes 359428
  7.2 8.7 %copy-start.7 = (f32[384]{0:T(512)S(1)}, f32[384]{0:T(512)}, u32[]{:S(2)}) copy-start(f32[384]{0:T(512)} %param.17) | copy-start | bytes 4612
  7.2 221.2 %all-reduce.3.cloned.1.call-start = ((), (), s32[]{:S(2)}) async-start(), calls=%async_computation | async-start | bytes 5242880 | tf_op jit(solution)/shard_map/psum | solution.py:19
  10.3 82.4 %collective-permute-start = (bf16[2,256,2560]{1,2,0:T(8,128)(2,1)S(1)}, bf16[2,256,2560]{1,2,0:T(8,128)(2,1)}, u32[]{:S(2)}, u32[]{:S(2)}) collective-permute-start(bf16[2,256,2560]{1,2,0:T(8,128)(2,1)S(1)} %copy.34), channel_id=1, source_target_pairs={{0,1},{1,2},{2,3},{3,4},{4,5},{5,6},{6,7},{7,8},{8,9},{9,10},{10,1... | collective-permute-start | bytes 7864328 | tf_op jit(solution)/shard_map/ppermute | solution.py:14
  10.8 85.4 %collective-permute-start.1 = (bf16[2,256,2560]{1,2,0:T(8,128)(2,1)S(1)}, bf16[2,256,2560]{1,2,0:T(8,128)(2,1)}, u32[]{:S(2)}, u32[]{:S(2)}) collective-permute-start(bf16[2,256,2560]{1,2,0:T(8,128)(2,1)S(1)} %copy.34), channel_id=1, source_target_pairs={{0,2},{1,3},{2,4},{3,5},{4,6},{5,7},{6,8},{7,9},{8,10},{9,11},{10,... | collective-permute-start | bytes 7864328 | tf_op jit(solution)/shard_map/ppermute | solution.py:14
  13.3 125.0 %collective-permute-start.2 = (bf16[2,256,2560]{1,2,0:T(8,128)(2,1)S(1)}, bf16[2,256,2560]{1,2,0:T(8,128)(2,1)}, u32[]{:S(2)}, u32[]{:S(2)}) collective-permute-start(bf16[2,256,2560]{1,2,0:T(8,128)(2,1)S(1)} %copy.34), channel_id=1, source_target_pairs={{0,3},{1,4},{2,5},{3,6},{4,7},{5,8},{6,9},{7,10},{8,11},{9,12},{10... | collective-permute-start | bytes 7864328 | tf_op jit(solution)/shard_map/ppermute | solution.py:14
  16.8 26.8 %collective-permute-start.4 = (bf16[5,1,52,384]{3,2,0,1:T(8,128)(2,1)}, bf16[5,1,52,384]{3,2,0,1:T(8,128)(2,1)S(1)}, u32[]{:S(2)}, u32[]{:S(2)}) collective-permute-start(bf16[5,1,52,384]{3,2,0,1:T(8,128)(2,1)} %pad_maximum_fusion), channel_id=1, source_target_pairs={{1,0},{2,1},{3,2},{4,3},{5,4},{6,5},{7,6},{8,7},{9,8},{10,9},{11,1... | collective-permute-start | bytes 599048 | tf_op jit(solution)/shard_map/ppermute | solution.py:30
  18.1 25.5 %collective-permute-start.3 = (bf16[5,1,52,384]{3,2,0,1:T(8,128)(2,1)}, bf16[5,1,52,384]{3,2,0,1:T(8,128)(2,1)S(1)}, u32[]{:S(2)}, u32[]{:S(2)}) collective-permute-start(bf16[5,1,52,384]{3,2,0,1:T(8,128)(2,1)} %pad_maximum_fusion), channel_id=1, source_target_pairs={{0,1},{1,2},{2,3},{3,4},{4,5},{5,6},{6,7},{7,8},{8,9},{9,10},{10,1... | collective-permute-start | bytes 599048 | tf_op jit(solution)/shard_map/ppermute | solution.py:27
  25.1 4.3 %copy-start.6 = (s32[16]{0:T(128)S(1)}, s32[16]{0:T(128)}, u32[]{:S(2)}) copy-start(s32[16]{0:T(128)} %param.14) | copy-start | bytes 196
  25.1 5.5 %copy-start.9 = (s32[16,3]{0,1:T(4,128)S(1)}, s32[16,3]{0,1:T(4,128)}, u32[]{:S(2)}) copy-start(s32[16,3]{0,1:T(4,128)} %param.13) | copy-start | bytes 580
  43.9 1.1 copy-start.8
  231.9 9.1 %copy-start.1 = (bf16[256,512]{0,1:T(8,128)(2,1)S(1)}, bf16[256,512]{0,1:T(8,128)(2,1)}, u32[]{:S(2)}) copy-start(bf16[256,512]{0,1:T(8,128)(2,1)} %copy.78) | copy-start | bytes 786436
  243.0 5.6 %copy-start.3 = (bf16[256,512]{0,1:T(8,128)(2,1)S(1)}, bf16[256,512]{0,1:T(8,128)(2,1)}, u32[]{:S(2)}) copy-start(bf16[256,512]{0,1:T(8,128)(2,1)} %copy.79) | copy-start | bytes 786436
  248.6 3.3 %copy-start.4 = (bf16[256,512]{0,1:T(8,128)(2,1)S(1)}, bf16[256,512]{0,1:T(8,128)(2,1)}, u32[]{:S(2)}) copy-start(bf16[256,512]{0,1:T(8,128)(2,1)} %copy.79) | copy-start | bytes 786436
  252.0 6.0 %copy-start.2 = (bf16[256,512]{0,1:T(8,128)(2,1)S(1)}, bf16[256,512]{0,1:T(8,128)(2,1)}, u32[]{:S(2)}) copy-start(bf16[256,512]{0,1:T(8,128)(2,1)} %copy.80) | copy-start | bytes 786436
Sparse Core Ops, SparseCore 0:
  25.2 203.1 all-reduce.2
where the time goes:
time: 296 us; the launch traced here: 295 us
  waiting for transfers between devices  167 us (56%)
  local copies, waits for them, and re-layouts  47.7 us (16%)
  matrix products  44.5 us (15%)
  between operations  17.1 us (6%)
  starting transfers between devices  9.86 us (3%)
  other arithmetic  9.04 us (3%)
    psum x1, waiting for transfers between devices, spread(): return lax.psum(block, axis)  86.6 us
    ppermute x3, waiting for transfers between devices, from_behind(): return lax.ppermute(value, axis, pairs)  80.2 us
    unnamed x61, local copies, waits for them, and re-layouts  25.3 us
    dot_general x5, matrix products, shards(): jnp.einsum('hqk,khd->qhd', probs, value_group, preferred_element_type=jnp...  23.7 us
    sub x5, matrix products, shards(): weights = jnp.exp(scores - row_max)  14.8 us
    slice x1, local copies, waits for them, and re-layouts, shards(): key_group = gathered[0, :, first_col:last_col].reshape(-1, 4, DH)  9.06 us
    reshape x5, local copies, waits for them, and re-layouts, shards(): pieces.append(blended.reshape(tok_rows, 4 * DH))  6.15 us
    dot_general x1, matrix products, shards(): jnp.dot(columns, conv_weight.reshape(27 * channels, channels), preferred_...  5.99 us
  transfers between devices with their start and end apart: 6, of which 3 were waited for; matrix products, arithmetic and copies ran while one was open for 13% of the time, Pallas kernels for 0%

commit v1 on v0

--- a/solution.py
+++ b/solution.py
@@ -1,22 +1,283 @@
+import functools
+
 import jax
 import jax.numpy as jnp
 from jax import lax
+from jax.experimental import pallas as pl
+from jax.experimental.pallas import tpu as pltpu
 from jax.sharding import PartitionSpec as P
 
-H = 20
 DH = 128
 WIN = 4
-
-
-def from_behind(value, axis, steps):
-    count = lax.axis_size(axis)
-    pairs = [(source, (source + steps) % count) for source in range(count)]
-    return lax.ppermute(value, axis, pairs)
-
-
-def spread(block, axis, source):
-    block = jnp.where(lax.axis_index(axis) == source, block, jnp.zeros_like(block))
-    return lax.psum(block, axis)
+PIECES = 10
+AHEAD = 4
+LOG2E = 1.4426950408889634
+MESH = pl.DeviceIdType.MESH
+
+
+def attention_kernel(
+    n, owner_ref, q_ref, kv_ref, bias_ref, out_ref, slots, up_in, down_in, up_out, down_out, recv, send
+):
+    rows = n // 4
+    width = q_ref.shape[1] // PIECES
+    me = lax.axis_index("span")
+    role = lax.rem(me, 4)
+    z = me // 4
+
+    def at(offset):
+        return lax.rem(me + offset + n, n)
+
+    def columns(piece):
+        return pl.ds(pl.multiple_of(piece * width, width), width)
+
+    def own(piece):
+        return kv_ref.at[:, :, columns(piece)]
+
+    def to_slot(source, slot, piece, lane, offset):
+        return pltpu.make_async_remote_copy(
+            src_ref=source,
+            dst_ref=slots.at[slot, piece],
+            send_sem=send.at[lane, piece],
+            recv_sem=recv.at[slot, piece],
+            device_id={"span": at(offset)},
+            device_id_type=MESH,
+        )
+
+    def wave(source, target, kind, piece, offset):
+        return pltpu.make_async_remote_copy(
+            src_ref=source.at[piece],
+            dst_ref=target.at[piece],
+            send_sem=send.at[kind, piece],
+            recv_sem=recv.at[kind, piece],
+            device_id={"span": at(offset)},
+            device_id_type=MESH,
+        )
+
+    def arrived(slot, piece):
+        to_slot(slots.at[slot, piece], slot, piece, 0, 1).wait_recv()
+
+    barrier = pltpu.get_barrier_semaphore()
+    for offset in (-4, -3, -2, -1, 1, 2, 3, 4):
+        pl.semaphore_signal(barrier, inc=1, device_id={"span": at(offset)}, device_id_type=MESH)
+    pl.semaphore_wait(barrier, 8)
+
+    direct = {
+        0: ((1, 1, 2), (0, 0, 1)),
+        1: ((2, 0, 3), (1, 1, 2)),
+        2: ((1, 1, 2), (0, 0, 1)),
+        3: ((2, 0, 3),),
+    }
+
+    def send_own(piece):
+        for which, copies in direct.items():
+
+            @pl.when(role == which)
+            def _():
+                for slot, lane, offset in copies:
+                    to_slot(own(piece), slot, piece, lane, offset).start()
+
+    passed = {
+        0: ((1, 2, 2, 1), (0, 1, 3, 1)),
+        2: ((2, 0, 2, -2), (1, 2, 3, 1)),
+        3: ((1, 0, 2, -1),),
+    }
+    kept = {0: (2,), 1: (0, 1, 2), 2: (0,), 3: (0, 2)}
+
+    def window(piece):
+        for which in range(4):
+
+            @pl.when(role == which)
+            def _():
+                for slot, there, lane, offset in passed.get(which, ()):
+                    arrived(slot, piece)
+                    to_slot(slots.at[slot, piece], there, piece, lane, offset).start()
+                for slot in kept[which]:
+                    arrived(slot, piece)
+
+    anchor = owner_ref[0]
+    behind = lax.rem(me - anchor + n, n)
+    group = jnp.where(role == 0, lax.rem((anchor + 3) // 4, rows), anchor // 4)
+
+    def mine(piece, part):
+        value = jnp.where(behind == 2, slots[1, piece, part], slots[2, piece, part])
+        value = jnp.where(behind == 1, slots[0, piece, part], value)
+        return jnp.where(behind == 0, kv_ref[part, :, columns(piece)], value)
+
+    def crosses(piece):
+        return lax.rem(piece, 2) == 1
+
+    def waves(piece):
+        return (role == 3) | ((role == 0) & jnp.logical_not(crosses(piece)))
+
+    def within(piece):
+        return (piece >= 0) & (piece < PIECES)
+
+    def attend(piece):
+        for sub in range(width // DH):
+            cols = pl.ds(pl.multiple_of(piece * width + sub * DH, DH), DH)
+            inner = slice(sub * DH, (sub + 1) * DH)
+            query = q_ref[:, cols]
+            scores = []
+            for block in range(5):
+                key = kv_ref[0, :, cols] if block == 0 else slots[block - 1, piece, 0, :, inner]
+                score = lax.dot_general(
+                    query, key, (((1,), (1,)), ((), ())), preferred_element_type=jnp.float32
+                )
+                scores.append(score * (DH**-0.5 * LOG2E) + bias_ref[block : block + 1, :])
+            top = functools.reduce(jnp.maximum, scores)
+            top = jnp.max(top, axis=-1, keepdims=True)
+            weights = [jnp.exp2(score - top) for score in scores]
+            total = jnp.sum(functools.reduce(jnp.add, weights), axis=-1, keepdims=True)
+            blended = None
+            for block in range(5):
+                value = kv_ref[1, :, cols] if block == 0 else slots[block - 1, piece, 1, :, inner]
+                term = jnp.dot(
+                    weights[block].astype(jnp.bfloat16), value, preferred_element_type=jnp.float32
+                )
+                blended = term if blended is None else blended + term
+            out_ref[:, cols] = (blended / total).astype(out_ref.dtype)
+
+    def start(piece, _):
+        send_own(piece)
+        return 0
+
+    lax.fori_loop(0, AHEAD, start, 0)
+
+    def step(t, _):
+        @pl.when(t + AHEAD < PIECES)
+        def _():
+            send_own(t + AHEAD)
+
+        @pl.when(t < PIECES)
+        def _():
+            window(t)
+
+        rising = t - z
+        falling = t - (rows - 1 - z)
+        final = t - (rows - 1)
+        ready = t - rows
+
+        @pl.when(within(rising) & waves(rising))
+        def _():
+            @pl.when(z > 0)
+            def _():
+                wave(up_out, up_in, 4, rising, 4).wait_recv()
+
+            @pl.when(z < rows - 1)
+            def _():
+                for part in range(2):
+                    up_out[rising, part] = jnp.where(
+                        group == z, mine(rising, part), up_in[rising, part]
+                    )
+                wave(up_out, up_in, 4, rising, 4).start()
+
+        @pl.when(within(falling) & waves(falling))
+        def _():
+            @pl.when(z < rows - 1)
+            def _():
+                wave(down_out, down_in, 5, falling, -4).wait_recv()
+
+            @pl.when(z > 0)
+            def _():
+                for part in range(2):
+                    down_out[falling, part] = jnp.where(
+                        group == z, mine(falling, part), down_in[falling, part]
+                    )
+                wave(down_out, down_in, 5, falling, -4).start()
+
+        @pl.when(within(final) & waves(final))
+        def _():
+            for part in range(2):
+                value = jnp.where(group < z, up_in[final, part], down_in[final, part])
+                slots[3, final, part] = jnp.where(group == z, mine(final, part), value)
+
+            @pl.when((role == 3) & crosses(final))
+            def _():
+                to_slot(slots.at[3, final], 3, final, 7, -3).start()
+
+            @pl.when(role == 3)
+            def _():
+                to_slot(slots.at[3, final], 3, final, 6, -1).start()
+
+            @pl.when(role == 0)
+            def _():
+                to_slot(slots.at[3, final], 3, final, 6, 1).start()
+
+        @pl.when(within(ready))
+        def _():
+            @pl.when((role == 0) & crosses(ready))
+            def _():
+                arrived(3, ready)
+                to_slot(slots.at[3, ready], 3, ready, 6, 1).start()
+
+            @pl.when((role == 1) | (role == 2))
+            def _():
+                arrived(3, ready)
+
+            attend(ready)
+
+        return 0
+
+    lax.fori_loop(0, PIECES + rows, step, 0)
+
+    def finish(piece, _):
+        for which in range(4):
+
+            @pl.when(role == which)
+            def _():
+                for slot, lane, offset in direct[which]:
+                    to_slot(own(piece), slot, piece, lane, offset).wait_send()
+                for slot, there, lane, offset in passed.get(which, ()):
+                    to_slot(slots.at[slot, piece], there, piece, lane, offset).wait_send()
+
+        @pl.when(waves(piece) & (z < rows - 1))
+        def _():
+            wave(up_out, up_in, 4, piece, 4).wait_send()
+
+        @pl.when(waves(piece) & (z > 0))
+        def _():
+            wave(down_out, down_in, 5, piece, -4).wait_send()
+
+        @pl.when((role == 0) | (role == 3))
+        def _():
+            to_slot(slots.at[3, piece], 3, piece, 6, 1).wait_send()
+
+        @pl.when((role == 3) & crosses(piece))
+        def _():
+            to_slot(slots.at[3, piece], 3, piece, 7, -3).wait_send()
+
+        return 0
+
+    lax.fori_loop(0, PIECES, finish, 0)
+
+
+def attention(queries, keys_values, owner, bias):
+    n = lax.axis_size("span")
+    rows, cols = queries.shape
+    piece = (PIECES, 2, rows, cols // PIECES)
+    flops = 4 * rows * 5 * rows * cols
+    return pl.pallas_call(
+        functools.partial(attention_kernel, n),
+        out_shape=jax.ShapeDtypeStruct((rows, cols), jnp.bfloat16),
+        in_specs=[pl.BlockSpec(memory_space=pltpu.SMEM)] + [pl.BlockSpec(memory_space=pltpu.VMEM)] * 3,
+        out_specs=pl.BlockSpec(memory_space=pltpu.VMEM),
+        scratch_shapes=[
+            pltpu.VMEM((4,) + piece, jnp.bfloat16),
+            pltpu.VMEM(piece, jnp.bfloat16),
+            pltpu.VMEM(piece, jnp.bfloat16),
+            pltpu.VMEM(piece, jnp.bfloat16),
+            pltpu.VMEM(piece, jnp.bfloat16),
+            pltpu.SemaphoreType.DMA((6, PIECES)),
+            pltpu.SemaphoreType.DMA((8, PIECES)),
+        ],
+        cost_estimate=pl.CostEstimate(
+            flops=flops, bytes_accessed=8 * rows * cols, transcendentals=5 * rows * rows * cols // DH
+        ),
+        compiler_params=pltpu.CompilerParams(
+            collective_id=0, has_side_effects=True, vmem_limit_bytes=52 * 1024 * 1024
+        ),
+        name="span_attention",
+    )(owner, queries, keys_values, bias)
 
 
 def extended_2(block, sides, width):
@@ -50,37 +311,15 @@
     position = (place - anchor - 1) % devices
     tok_rows = queries.shape[0]
     row_ids = jnp.arange(tok_rows, dtype=jnp.int32)
-    blocks = [keys_values]
     valid_list = [row_ids < lengths[place]]
-    for offset in range(1, WIN):
-        blocks.append(from_behind(keys_values, "span", offset))
     for offset in range(1, WIN):
         source = (place - offset) % devices
         allowed = (position >= offset) & (span_mask[position, offset - 1] == 1)
         valid_list.append(allowed & (row_ids < lengths[source]))
-    blocks.append(spread(keys_values, "span", anchor))
     valid_list.append((place != anchor) & (row_ids < lengths[anchor]))
-    gathered = jnp.concatenate(blocks, axis=1)
-    key_valid = jnp.concatenate(valid_list)
-    score_scale = DH ** (-0.5)
-    pieces = []
-    for head_block in range(H // 4):
-        first_col = head_block * 4 * DH
-        last_col = first_col + 4 * DH
-        query_group = queries[:, first_col:last_col].reshape(tok_rows, 4, DH)
-        key_group = gathered[0, :, first_col:last_col].reshape(-1, 4, DH)
-        value_group = gathered[1, :, first_col:last_col].reshape(-1, 4, DH)
-        scores = (
-            jnp.einsum("qhd,khd->hqk", query_group, key_group, preferred_element_type=jnp.float32)
-            * score_scale
-        )
-        scores = jnp.where(key_valid[None, None, :], scores, -jnp.inf)
-        row_max = jnp.max(scores, axis=-1, keepdims=True)
-        weights = jnp.exp(scores - row_max)
-        probs = (weights / jnp.sum(weights, axis=-1, keepdims=True)).astype(jnp.bfloat16)
-        blended = jnp.einsum("hqk,khd->qhd", probs, value_group, preferred_element_type=jnp.float32)
-        pieces.append(blended.reshape(tok_rows, 4 * DH))
-    attended = jnp.concatenate(pieces, axis=1)
+    bias = jnp.where(jnp.stack(valid_list), 0.0, -1e30).astype(jnp.float32)
+    bias = jnp.pad(bias, ((0, 3), (0, 0)))
+    attended = attention(queries, keys_values, owner, bias)
     attended = jnp.where(row_ids[:, None] < lengths[place], attended, 0.0).astype(jnp.bfloat16)
     features = frames.astype(jnp.float32)
     squares = jnp.mean(features * features, axis=-1, keepdims=True)

time: 296 us -> 141 us (0.48)
  waiting for transfers between devices: 167 us -> 0.01 us
  Pallas kernels: 0 us -> 117 us
  local copies, waits for them, and re-layouts: 47.7 us -> 4.68 us
  matrix products: 44.5 us -> 2.76 us
  between operations: 17.1 us -> 3.55 us
  starting transfers between devices: 9.86 us -> 3.66 us
    pallas_call x0 -> x1, Pallas kernels: none -> 117 us  [attention(): pl.pallas_call(functools.partial(attention_kernel, n), out_shape=jax.Shap...]
    psum x1 -> x0, waiting for transfers between devices: 86.6 us -> none  [spread(): return lax.psum(block, axis)]
    ppermute x3 -> x0, waiting for transfers between devices: 80.2 us -> none  [from_behind(): return lax.ppermute(value, axis, pairs)]
    dot_general x5 -> x0, matrix products: 23.7 us -> none  [shards(): jnp.einsum('hqk,khd->qhd', probs, value_group, preferred_element_type=jnp...]
    unnamed x61 -> x34, local copies, waits for them, and re-layouts: 25.3 us -> 1.64 us
    sub x5 -> x0, matrix products: 14.8 us -> none  [shards(): weights = jnp.exp(scores - row_max)]
    slice x2 -> x0, local copies, waits for them, and re-layouts: 11.4 us -> none  [the longest x1 9.06 us: shards(): key_group = gathered[0, :, first_col:last_col].reshape(-1, 4, DH)]
    reshape x5 -> x0, local copies, waits for them, and re-layouts: 6.15 us -> none  [shards(): pieces.append(blended.reshape(tok_rows, 4 * DH))]
  transfers between devices with their start and end apart: 6 -> 2, of which waited for: 3 -> 0; matrix products, arithmetic and copies ran while one was open for 13% -> 6% of each run, Pallas kernels for 0% -> 84%
where the time goes in v1:
time: 141 us; the launch traced here: 139 us
  Pallas kernels  117 us (83%)
  other arithmetic  7.47 us (5%)
  local copies, waits for them, and re-layouts  4.68 us (3%)
  starting transfers between devices  3.66 us (3%)
  between operations  3.55 us (3%)
  matrix products  2.76 us (2%)
    pallas_call x1, Pallas kernels, attention(): pl.pallas_call(functools.partial(attention_kernel, n), out_shape=jax.Shap...  117 us
  transfers between devices with their start and end apart: 2, of which 0 were waited for; matrix products, arithmetic and copies ran while one was open for 6% of the time, Pallas kernels for 84%

profile of v1, /device:TPU:0, one launch (start us, length us, event | category | flops | bytes accessed | tf_op | source)
XLA Modules:
  0.0 139.4 jit_solution(12212593471435845140)
XLA Ops:
  0.6 1.0 fusion.18
  1.7 0.9 copy.13
  2.6 1.1 fusion.25
  3.7 2.4 %collective-permute-start = (bf16[5,1,52,384]{3,2,0,1:T(8,128)(2,1)S(1)}, bf16[5,1,52,384]{3,2,0,1:T(8,128)(2,1)S(1)}, u32[]{:S(2)}, u32[]{:S(2)}) collective-permute-start(bf16[5,1,52,384]{3,2,0,1:T(8,128)(2,1)S(1)} %pad_maximum_fusion), channel_id=1, source_target_pairs={{0,1},{1,2},{2,3},{3,4},{4,5},{5,6},{6,7},{7,8},{8,9},{9,10},{10,1... | collective-permute-start | bytes 599048 | tf_op jit(solution)/shard_map/ppermute | solution.py:288
  6.0 1.3 collective-permute-start.1
  8.1 1.5 %fusion.30 = (s32[1]{0:T(128)}, s32[1]{0:T(128)}, s32[1]{0:T(128)}, s32[1]{0:T(128)}, s32[1]{0:T(128)}) fusion(s32[16]{0:T(128)} %param.14, s32[]{:T(128)S(6)} %select_n.57, s32[]{:T(128)S(6)} %select_n.54, s32[]{:T(128)S(6)} %select_n.52, s32[]{:T(128)S(6)} %select_n.48, s32[]{:T(128)S(6)} %select_n.56), kind=kLoop, calls=%fused_computation.71 | loop fusion | bytes 60 | tf_op jit(solution)/shard_map/dynamic_slice | solution.py:319
  9.6 0.6 iota_compare_fusion.2
  10.2 0.6 iota_compare_fusion.3
  10.8 1.4 %constant_dynamic-slice_fusion = (s32[1,1]{0,1:T(1,128)}, s32[1,1]{0,1:T(1,128)}, s32[1,1]{0,1:T(1,128)}) fusion(s32[16,3]{0,1:T(4,128)} %param.13, s32[]{:T(128)S(6)} %select_n.50), kind=kLoop, calls=%fused_computation.68 | loop fusion | bytes 28 | tf_op jit(solution)/shard_map/dynamic_slice | solution.py:317
  14.0 1.3 compare_and_fusion
  15.3 1.3 compare_and_fusion.2
  16.6 0.0 slice-start
  16.7 0.0 slice-start.1
  16.7 117.2 %span_attention.1 = bf16[256,2560]{1,0:T(8,128)(2,1)S(1)} custom-call(s32[1]{0:T(128)} %copy.41.owner_ref, bf16[256,2560]{1,0:T(8,128)(2,1)} %q_ref.1, bf16[2,256,2560]{2,1,0:T(8,128)(2,1)} %kv_ref.1, f32[8,256]{1,0:T(8,128)S(1)} %pad.8.bias_ref), custom_call_target="tpu_custom_call" | custom-call | flops 3355443200 | bytes 5242880 | tf_op jit(solution)/shard_map/span_attention/pallas_call | solution.py:259
  133.9 1.2 broadcast_select_fusion
  135.1 0.0 copy-start
  135.1 0.0 copy-start.1
  135.1 0.0 collective-permute-done
  135.1 0.0 collective-permute-done.1
  135.2 0.2 select_maximum_fusion
  135.4 0.0 copy-start.2
  136.2 0.0 copy-done
  136.2 0.0 copy-done.1
  136.2 0.2 constant_dynamic-update-slice_fusion
  136.6 0.0 slice-done
  136.6 0.0 slice-done.1
  136.6 0.0 copy-done.2
  136.6 2.8 %fusion.12 = bf16[3,1,52,384]{3,2,1,0:T(8,128)(2,1)} fusion(bf16[10368,384,1]{1,0,2:T(8,128)(2,1)S(1)} %bitcast.47, bf16[3,1,52,10368]{3,2,0,1:T(8,128)(2,1)S(1)} %slice_dynamic-update-slice_fusion, bf16[3,1,52,384]{3,2,1,0:T(8,128)(2,1)S(1)} %copy-done, f32[384]{0:T(512)S(1)} %copy-done.2), kind=kOutput, calls=%fused_computation.9 | convolution fusion | flops 1242408960 | bytes 11438592 | tf_op jit(solution)/shard_map/dot_general | solution.py:348
  (32 shorter events, 0.9 us)
Async XLA Ops:
  3.7 131.5 %collective-permute-start = (bf16[5,1,52,384]{3,2,0,1:T(8,128)(2,1)S(1)}, bf16[5,1,52,384]{3,2,0,1:T(8,128)(2,1)S(1)}, u32[]{:S(2)}, u32[]{:S(2)}) collective-permute-start(bf16[5,1,52,384]{3,2,0,1:T(8,128)(2,1)S(1)} %pad_maximum_fusion), channel_id=1, source_target_pairs={{0,1},{1,2},{2,3},{3,4},{4,5},{5,6},{6,7},{7,8},{8,9},{9,10},{10,1... | collective-permute-start | bytes 599048 | tf_op jit(solution)/shard_map/ppermute | solution.py:288
  6.0 129.1 %collective-permute-start.1 = (bf16[5,1,52,384]{3,2,0,1:T(8,128)(2,1)S(1)}, bf16[5,1,52,384]{3,2,0,1:T(8,128)(2,1)S(1)}, u32[]{:S(2)}, u32[]{:S(2)}) collective-permute-start(bf16[5,1,52,384]{3,2,0,1:T(8,128)(2,1)S(1)} %pad_maximum_fusion), channel_id=1, source_target_pairs={{1,0},{2,1},{3,2},{4,3},{5,4},{6,5},{7,6},{8,7},{9,8},{10,9},{11,1... | collective-permute-start | bytes 599048 | tf_op jit(solution)/shard_map/ppermute | solution.py:291
  16.6 119.9 %slice-start = ((s8[7962624]{0:T(1024)(128)(4,1)}), s8[4194304]{0:T(1024)(128)(4,1)S(1)}, s32[]{:S(2)}) async-start(s8[7962624]{0:T(1024)(128)(4,1)} %bitcast.45), calls=%async_computation | async-start | bytes 8388608
  16.7 119.9 %slice-start.1 = ((s8[7962624]{0:T(1024)(128)(4,1)}), s8[3768320]{0:T(1024)(128)(4,1)S(1)}, s32[]{:S(2)}) async-start(s8[7962624]{0:T(1024)(128)(4,1)} %bitcast.45), calls=%async_computation.1 | async-start | bytes 7536640
  135.1 1.1 copy-start
  135.1 1.1 copy-start.1
  135.4 1.2 copy-start.2

commit v2 on v1

--- a/solution.py
+++ b/solution.py
@@ -15,9 +15,38 @@
 MESH = pl.DeviceIdType.MESH
 
 
-def attention_kernel(
-    n, owner_ref, q_ref, kv_ref, bias_ref, out_ref, slots, up_in, down_in, up_out, down_out, recv, send
+def block_kernel(
+    n,
+    owner_ref,
+    mask_ref,
+    lengths_ref,
+    q_ref,
+    kv_ref,
+    frames_ref,
+    past_ref,
+    gain_ref,
+    shift_ref,
+    weight_ref,
+    out_ref,
+    decoded_ref,
+    slots,
+    up_in,
+    down_in,
+    up_out,
+    down_out,
+    taps,
+    weights_here,
+    partial,
+    recv,
+    send,
+    edge_recv,
+    edge_send,
+    weight_sem,
 ):
+    tokens = q_ref.shape[0]
+    frames, _, cols, channels = frames_ref.shape
+    past = past_ref.shape[0]
+    padded = taps.shape[2]
     rows = n // 4
     width = q_ref.shape[1] // PIECES
     me = lax.axis_index("span")
@@ -56,6 +85,19 @@
     def arrived(slot, piece):
         to_slot(slots.at[slot, piece], slot, piece, 0, 1).wait_recv()
 
+    def edge(which):
+        return pltpu.make_async_remote_copy(
+            src_ref=taps.at[1],
+            dst_ref=taps.at[2 * which],
+            send_sem=edge_send.at[which],
+            recv_sem=edge_recv.at[which],
+            device_id={"span": at(1 - 2 * which)},
+            device_id_type=MESH,
+        )
+
+    weight_copy = pltpu.make_async_copy(weight_ref, weights_here, weight_sem)
+    weight_copy.start()
+
     barrier = pltpu.get_barrier_semaphore()
     for offset in (-4, -3, -2, -1, 1, 2, 3, 4):
         pl.semaphore_signal(barrier, inc=1, device_id={"span": at(offset)}, device_id_type=MESH)
@@ -112,7 +154,80 @@
     def within(piece):
         return (piece >= 0) & (piece < PIECES)
 
+    position = lax.rem(me - anchor - 1 + 2 * n, n)
+    length = lengths_ref[me]
+    limits = [length]
+    for offset in range(1, WIN):
+        allowed = (position >= offset) & (mask_ref[position, offset - 1] == 1)
+        limits.append(jnp.where(allowed, lengths_ref[at(-offset)], 0))
+    limits.append(jnp.where(behind == 0, 0, lengths_ref[anchor]))
+
+    def activate():
+        spare = partial.at[0, 0, 0:padded, :]
+        for frame in range(past + frames):
+            if frame < past:
+                value = past_ref[frame, 0].astype(jnp.float32)
+            else:
+                value = frames_ref[frame - past, 0].astype(jnp.float32)
+                squares = jnp.mean(value * value, axis=-1, keepdims=True)
+                value = value * lax.rsqrt(squares + 1e-06) * gain_ref[...]
+                value = value / (1.0 + jnp.exp(-value))
+            spare[...] = jnp.zeros(spare.shape, jnp.float32)
+            spare[0:cols, :] = value
+            taps[1, frame] = spare[...].astype(jnp.bfloat16)
+        partial[0, :, 0:8, :] = jnp.zeros((frames, 8, channels), jnp.float32)
+
+        @pl.when(me < n - 1)
+        def _():
+            edge(0).start()
+
+        @pl.when(me > 0)
+        def _():
+            edge(1).start()
+
+        @pl.when(me == 0)
+        def _():
+            taps[0] = jnp.zeros(taps.shape[1:], taps.dtype)
+
+        @pl.when(me == n - 1)
+        def _():
+            taps[2] = jnp.zeros(taps.shape[1:], taps.dtype)
+
+    def edges_arrived():
+        @pl.when(me > 0)
+        def _():
+            edge(0).wait_recv()
+
+        @pl.when(me < n - 1)
+        def _():
+            edge(1).wait_recv()
+
+        weight_copy.wait()
+
+    def convolve(col_tap):
+        total = None
+        for frame_tap in range(3):
+            for row_tap in range(3):
+                window_rows = taps[row_tap, frame_tap : frame_tap + frames]
+                term = jnp.dot(
+                    window_rows.reshape(frames * padded, channels),
+                    weights_here[frame_tap, row_tap, col_tap],
+                    preferred_element_type=jnp.float32,
+                )
+                total = term if total is None else total + term
+        partial[col_tap, :, 8 : 8 + padded, :] = total.reshape(frames, padded, channels)
+
+    def decode():
+        for frame in range(frames):
+            total = frames_ref[frame, 0].astype(jnp.float32) + shift_ref[...]
+            for col_tap in range(3):
+                total = total + partial[col_tap, frame, 7 + col_tap : 7 + col_tap + cols, :]
+            decoded_ref[frame, 0] = total.astype(decoded_ref.dtype)
+
     def attend(piece):
+        token = lax.broadcasted_iota(jnp.int32, (1, tokens), 1)
+        hidden = [jnp.where(token < limit, 0.0, -1e30) for limit in limits]
+        row = lax.broadcasted_iota(jnp.int32, (tokens, 1), 0)
         for sub in range(width // DH):
             cols = pl.ds(pl.multiple_of(piece * width + sub * DH, DH), DH)
             inner = slice(sub * DH, (sub + 1) * DH)
@@ -123,7 +238,7 @@
                 score = lax.dot_general(
                     query, key, (((1,), (1,)), ((), ())), preferred_element_type=jnp.float32
                 )
-                scores.append(score * (DH**-0.5 * LOG2E) + bias_ref[block : block + 1, :])
+                scores.append(score * (DH**-0.5 * LOG2E) + hidden[block])
             top = functools.reduce(jnp.maximum, scores)
             top = jnp.max(top, axis=-1, keepdims=True)
             weights = [jnp.exp2(score - top) for score in scores]
@@ -135,13 +250,14 @@
                     weights[block].astype(jnp.bfloat16), value, preferred_element_type=jnp.float32
                 )
                 blended = term if blended is None else blended + term
-            out_ref[:, cols] = (blended / total).astype(out_ref.dtype)
+            out_ref[:, cols] = jnp.where(row < length, blended / total, 0.0).astype(out_ref.dtype)
 
     def start(piece, _):
         send_own(piece)
         return 0
 
     lax.fori_loop(0, AHEAD, start, 0)
+    activate()
 
     def step(t, _):
         @pl.when(t + AHEAD < PIECES)
@@ -151,6 +267,18 @@
         @pl.when(t < PIECES)
         def _():
             window(t)
+
+        @pl.when(t == 2)
+        def _():
+            edges_arrived()
+
+        @pl.when((t >= 2) & (t < 5))
+        def _():
+            convolve(t - 2)
+
+        @pl.when(t == 5)
+        def _():
+            decode()
 
         rising = t - z
         falling = t - (rows - 1 - z)
@@ -250,47 +378,13 @@
 
     lax.fori_loop(0, PIECES, finish, 0)
 
-
-def attention(queries, keys_values, owner, bias):
-    n = lax.axis_size("span")
-    rows, cols = queries.shape
-    piece = (PIECES, 2, rows, cols // PIECES)
-    flops = 4 * rows * 5 * rows * cols
-    return pl.pallas_call(
-        functools.partial(attention_kernel, n),
-        out_shape=jax.ShapeDtypeStruct((rows, cols), jnp.bfloat16),
-        in_specs=[pl.BlockSpec(memory_space=pltpu.SMEM)] + [pl.BlockSpec(memory_space=pltpu.VMEM)] * 3,
-        out_specs=pl.BlockSpec(memory_space=pltpu.VMEM),
-        scratch_shapes=[
-            pltpu.VMEM((4,) + piece, jnp.bfloat16),
-            pltpu.VMEM(piece, jnp.bfloat16),
-            pltpu.VMEM(piece, jnp.bfloat16),
-            pltpu.VMEM(piece, jnp.bfloat16),
-            pltpu.VMEM(piece, jnp.bfloat16),
-            pltpu.SemaphoreType.DMA((6, PIECES)),
-            pltpu.SemaphoreType.DMA((8, PIECES)),
-        ],
-        cost_estimate=pl.CostEstimate(
-            flops=flops, bytes_accessed=8 * rows * cols, transcendentals=5 * rows * rows * cols // DH
-        ),
-        compiler_params=pltpu.CompilerParams(
-            collective_id=0, has_side_effects=True, vmem_limit_bytes=52 * 1024 * 1024
-        ),
-        name="span_attention",
-    )(owner, queries, keys_values, bias)
-
-
-def extended_2(block, sides, width):
-    for axis, dim in sides:
-        count = lax.axis_size(axis)
-        forward = [(i, i + 1) for i in range(count - 1)]
-        backward = [(target, source) for source, target in forward]
-        low = lax.ppermute(
-            lax.slice_in_dim(block, block.shape[dim] - width, None, axis=dim), axis, forward
-        )
-        high = lax.ppermute(lax.slice_in_dim(block, 0, width, axis=dim), axis, backward)
-        block = jnp.concatenate([low, block, high], axis=dim)
-    return block
+    @pl.when(me < n - 1)
+    def _():
+        edge(0).wait_send()
+
+    @pl.when(me > 0)
+    def _():
+        edge(1).wait_send()
 
 
 def shards(
@@ -305,51 +399,59 @@
     conv_weight,
     conv_bias,
 ):
-    devices = lax.axis_size("span")
-    place = lax.axis_index("span")
-    anchor = owner[0]
-    position = (place - anchor - 1) % devices
-    tok_rows = queries.shape[0]
-    row_ids = jnp.arange(tok_rows, dtype=jnp.int32)
-    valid_list = [row_ids < lengths[place]]
-    for offset in range(1, WIN):
-        source = (place - offset) % devices
-        allowed = (position >= offset) & (span_mask[position, offset - 1] == 1)
-        valid_list.append(allowed & (row_ids < lengths[source]))
-    valid_list.append((place != anchor) & (row_ids < lengths[anchor]))
-    bias = jnp.where(jnp.stack(valid_list), 0.0, -1e30).astype(jnp.float32)
-    bias = jnp.pad(bias, ((0, 3), (0, 0)))
-    attended = attention(queries, keys_values, owner, bias)
-    attended = jnp.where(row_ids[:, None] < lengths[place], attended, 0.0).astype(jnp.bfloat16)
-    features = frames.astype(jnp.float32)
-    squares = jnp.mean(features * features, axis=-1, keepdims=True)
-    normed = features * lax.rsqrt(squares + 1e-06) * norm_gain
-    activated = jax.nn.silu(normed).astype(jnp.bfloat16)
-    stacked = jnp.concatenate([past_frames, activated], axis=0)
-    extended = extended_2(stacked, (("span", 1),), 1)
-    padded = jnp.pad(extended, ((0, 0), (0, 0), (1, 1), (0, 0)))
-    frame_count = frames.shape[0]
-    rows_here = frames.shape[1]
-    col_count = frames.shape[2]
-    channels = frames.shape[3]
-    windows = []
-    for frame_tap in range(3):
-        for row_tap in range(3):
-            for col_tap in range(3):
-                windows.append(
-                    padded[
-                        frame_tap : frame_tap + frame_count,
-                        row_tap : row_tap + rows_here,
-                        col_tap : col_tap + col_count,
-                        :,
-                    ]
-                )
-    columns = jnp.concatenate(windows, axis=-1).reshape(-1, 27 * channels)
-    convolved = jnp.dot(
-        columns, conv_weight.reshape(27 * channels, channels), preferred_element_type=jnp.float32
+    n = lax.axis_size("span")
+    rows, cols = queries.shape
+    piece = (PIECES, 2, rows, cols // PIECES)
+    frame_count, _, frame_cols, channels = frames.shape
+    padded = -(-(frame_cols + 1) // 16) * 16
+    attention_flops = 4 * rows * 5 * rows * cols
+    conv_flops = 2 * frame_count * frame_cols * conv_weight.size
+    scalars = pl.BlockSpec(memory_space=pltpu.SMEM)
+    whole = pl.BlockSpec(memory_space=pltpu.VMEM)
+    return pl.pallas_call(
+        functools.partial(block_kernel, n),
+        out_shape=(
+            jax.ShapeDtypeStruct((rows, cols), jnp.bfloat16),
+            jax.ShapeDtypeStruct(frames.shape, jnp.bfloat16),
+        ),
+        in_specs=[scalars] * 3 + [whole] * 6 + [pl.BlockSpec(memory_space=pl.ANY)],
+        out_specs=(whole, whole),
+        scratch_shapes=[
+            pltpu.VMEM((4,) + piece, jnp.bfloat16),
+            pltpu.VMEM(piece, jnp.bfloat16),
+            pltpu.VMEM(piece, jnp.bfloat16),
+            pltpu.VMEM(piece, jnp.bfloat16),
+            pltpu.VMEM(piece, jnp.bfloat16),
+            pltpu.VMEM((3, frame_count + past_frames.shape[0], padded, channels), jnp.bfloat16),
+            pltpu.VMEM(conv_weight.shape, jnp.bfloat16),
+            pltpu.VMEM((3, frame_count, padded + 16, channels), jnp.float32),
+            pltpu.SemaphoreType.DMA((6, PIECES)),
+            pltpu.SemaphoreType.DMA((8, PIECES)),
+            pltpu.SemaphoreType.DMA((2,)),
+            pltpu.SemaphoreType.DMA((2,)),
+            pltpu.SemaphoreType.DMA,
+        ],
+        cost_estimate=pl.CostEstimate(
+            flops=attention_flops + conv_flops,
+            bytes_accessed=8 * rows * cols + 2 * conv_weight.size,
+            transcendentals=5 * rows * rows * cols // DH,
+        ),
+        compiler_params=pltpu.CompilerParams(
+            collective_id=0, has_side_effects=True, vmem_limit_bytes=60 * 1024 * 1024
+        ),
+        name="spans_and_decoder",
+    )(
+        owner,
+        span_mask,
+        lengths,
+        queries,
+        keys_values,
+        frames,
+        past_frames,
+        norm_gain.reshape(1, channels),
+        conv_bias.reshape(1, channels),
+        conv_weight,
     )
-    decoded = features + conv_bias + convolved.reshape(frame_count, rows_here, col_count, channels)
-    return (attended, decoded.astype(jnp.bfloat16))
 
 
 def solution(mesh):

time: 141 us -> 131 us (0.929)
  other arithmetic: 7.47 us -> 0 us
  local copies, waits for them, and re-layouts: 4.68 us -> 8.55 us
  starting transfers between devices: 3.66 us -> 0 us
  Pallas kernels: 117 us -> 120 us
  matrix products: 2.76 us -> 0 us
  between operations: 3.55 us -> 1.3 us
    unnamed x34 -> x6, local copies, waits for them, and re-layouts: 1.64 us -> 6.03 us
    ppermute x2 -> x0, starting transfers between devices: 3.66 us -> none  [the longest x1 2.37 us: extended_2(): lax.ppermute(lax.slice_in_dim(block, block.shape[dim] - width, None, axis...]
    dynamic_slice x2 -> x0, local copies, waits for them, and re-layouts: 2.95 us -> none  [the longest x1 1.51 us: shards(): valid_list.append((place != anchor) & (row_ids < lengths[anchor]))]
    dot_general x1 -> x0, matrix products: 2.76 us -> none  [shards(): jnp.dot(columns, conv_weight.reshape(27 * channels, channels), preferred_...]
    and x2 -> x0, other arithmetic: 2.55 us -> none  [the longest x1 1.29 us: shards(): valid_list.append((place != anchor) & (row_ids < lengths[anchor]))]
    reshape x0 -> x2, local copies, waits for them, and re-layouts: none -> 2.52 us  [the longest x1 1.26 us: shards(): norm_gain.reshape(1, channels)]
    pallas_call x1, Pallas kernels: 117 us -> 120 us  [shards(): pl.pallas_call(functools.partial(block_kernel, n), out_shape=(jax.ShapeDt...]
  transfers between devices with their start and end apart: 2 -> 0, of which waited for: 0 -> 0; matrix products, arithmetic and copies ran while one was open for 6% -> 0% of each run, Pallas kernels for 84% -> 0%
where the time goes in v2:
time: 131 us; the launch traced here: 129 us
  Pallas kernels  120 us (92%)
  local copies, waits for them, and re-layouts  8.55 us (7%)
    pallas_call x1, Pallas kernels, shards(): pl.pallas_call(functools.partial(block_kernel, n), out_shape=(jax.ShapeDt...  120 us
    unnamed x6, local copies, waits for them, and re-layouts  6.03 us

profile of v2, /device:TPU:0, one launch (start us, length us, event | category | flops | bytes accessed | tf_op | source)
XLA Modules:
  0.0 129.4 jit_solution(15544032180414989582)
XLA Ops:
  1.3 1.3 reshape.10.gain_ref
  2.5 1.3 reshape.11.shift_ref
  3.8 1.4 %copy.12.mask_ref = s32[16,3]{1,0:T(8,128)} copy(s32[16,3]{0,1:T(4,128)} %param.13) | data formatting | bytes 384 | tf_op args[3]
  5.1 1.5 %copy.13.past_ref = bf16[2,1,52,384]{3,2,1,0:T(8,128)(2,1)} copy(bf16[2,1,52,384]{3,0,2,1:T(2,128)(2,1)} %param.16) | data formatting | bytes 159744 | tf_op args[6]
  6.7 119.6 %spans_and_decoder.1 = (bf16[256,2560]{1,0:T(8,128)(2,1)}, bf16[3,1,52,384]{3,2,1,0:T(8,128)(2,1)}) custom-call(s32[1]{0:T(128)S(6)} %copy.16.owner_ref, s32[16,3]{1,0:T(8,128)} %copy.12.mask_ref, s32[16]{0:T(128)} %lengths_ref.1, bf16[256,2560]{1,0:T(8,128)(2,1)} %q_ref.1, bf16[2,256,2560]{2,1,0:T(8,128)(2,1)} %kv_ref.1, ...), custom_call_target="tpu_custom_call" | custom-call | flops 4597612544 | bytes 13205504 | tf_op jit(solution)/shard_map/spans_and_decoder/pallas_call | solution.py:411
  126.3 0.0 copy-start
  126.3 2.5 %copy.17 = bf16[256,2560]{1,0:T(8,128)(2,1)} copy(bf16[256,2560]{1,0:T(8,128)(2,1)} %get-tuple-element.4) | data formatting | bytes 2621440
  128.8 0.0 copy-done
  128.8 0.7 copy.18
Async XLA Ops:
  126.3 2.5 %copy-start = (bf16[3,1,52,384]{3,2,1,0:T(8,128)(2,1)S(1)}, bf16[3,1,52,384]{3,2,1,0:T(8,128)(2,1)}, u32[]{:S(2)}) copy-start(bf16[3,1,52,384]{3,2,1,0:T(8,128)(2,1)} %get-tuple-element.5) | copy-start | bytes 359428

commit v3 on v2

--- a/solution.py
+++ b/solution.py
@@ -30,6 +30,7 @@
     out_ref,
     decoded_ref,
     slots,
+    relay,
     up_in,
     down_in,
     up_out,
@@ -106,11 +107,48 @@
     direct = {
         0: ((1, 1, 2), (0, 0, 1)),
         1: ((2, 0, 3), (1, 1, 2)),
-        2: ((1, 1, 2), (0, 0, 1)),
+        2: ((0, 0, 1),),
         3: ((2, 0, 3),),
     }
 
+    def even(piece):
+        return lax.rem(piece, 2) == 0
+
+    def to_relay(piece, offset):
+        return pltpu.make_async_remote_copy(
+            src_ref=own(piece),
+            dst_ref=relay.at[piece],
+            send_sem=send.at[1, piece],
+            recv_sem=recv.at[6, piece],
+            device_id={"span": at(offset)},
+            device_id_type=MESH,
+        )
+
+    def relayed(piece):
+        return ((role == 0) & even(piece)) | ((role == 2) & jnp.logical_not(even(piece)))
+
+    def pass_relayed(piece):
+        @pl.when(relayed(piece))
+        def _():
+            to_relay(piece, 1).wait_recv()
+
+        @pl.when((role == 0) & even(piece))
+        def _():
+            to_slot(relay.at[piece], 1, piece, 8, 4).start()
+
+        @pl.when((role == 2) & jnp.logical_not(even(piece)))
+        def _():
+            to_slot(relay.at[piece], 1, piece, 8, -2).start()
+
     def send_own(piece):
+        @pl.when((role == 2) & even(piece))
+        def _():
+            to_relay(piece, -2).start()
+
+        @pl.when((role == 2) & jnp.logical_not(even(piece)))
+        def _():
+            to_relay(piece, 4).start()
+
         for which, copies in direct.items():
 
             @pl.when(role == which)
@@ -126,6 +164,7 @@
     kept = {0: (2,), 1: (0, 1, 2), 2: (0,), 3: (0, 2)}
 
     def window(piece):
+        pass_relayed(piece)
         for which in range(4):
 
             @pl.when(role == which)
@@ -146,10 +185,14 @@
         return jnp.where(behind == 0, kv_ref[part, :, columns(piece)], value)
 
     def crosses(piece):
-        return lax.rem(piece, 2) == 1
+        return lax.rem(piece, 5) == 1
+
+    def crosses_back(piece):
+        return lax.rem(piece, 5) == 3
 
     def waves(piece):
-        return (role == 3) | ((role == 0) & jnp.logical_not(crosses(piece)))
+        upper = (role == 3) & jnp.logical_not(crosses_back(piece))
+        return upper | ((role == 0) & jnp.logical_not(crosses(piece)))
 
     def within(piece):
         return (piece >= 0) & (piece < PIECES)
@@ -170,7 +213,7 @@
             else:
                 value = frames_ref[frame - past, 0].astype(jnp.float32)
                 squares = jnp.mean(value * value, axis=-1, keepdims=True)
-                value = value * lax.rsqrt(squares + 1e-06) * gain_ref[...]
+                value = value * lax.rsqrt(squares + 1e-06) * gain_ref[...].reshape(1, channels)
                 value = value / (1.0 + jnp.exp(-value))
             spare[...] = jnp.zeros(spare.shape, jnp.float32)
             spare[0:cols, :] = value
@@ -219,7 +262,7 @@
 
     def decode():
         for frame in range(frames):
-            total = frames_ref[frame, 0].astype(jnp.float32) + shift_ref[...]
+            total = frames_ref[frame, 0].astype(jnp.float32) + shift_ref[...].reshape(1, channels)
             for col_tap in range(3):
                 total = total + partial[col_tap, frame, 7 + col_tap : 7 + col_tap + cols, :]
             decoded_ref[frame, 0] = total.astype(decoded_ref.dtype)
@@ -323,6 +366,10 @@
             def _():
                 to_slot(slots.at[3, final], 3, final, 7, -3).start()
 
+            @pl.when((role == 0) & crosses_back(final))
+            def _():
+                to_slot(slots.at[3, final], 3, final, 7, 3).start()
+
             @pl.when(role == 3)
             def _():
                 to_slot(slots.at[3, final], 3, final, 6, -1).start()
@@ -337,6 +384,11 @@
             def _():
                 arrived(3, ready)
                 to_slot(slots.at[3, ready], 3, ready, 6, 1).start()
+
+            @pl.when((role == 3) & crosses_back(ready))
+            def _():
+                arrived(3, ready)
+                to_slot(slots.at[3, ready], 3, ready, 6, -1).start()
 
             @pl.when((role == 1) | (role == 2))
             def _():
@@ -370,9 +422,17 @@
         def _():
             to_slot(slots.at[3, piece], 3, piece, 6, 1).wait_send()
 
-        @pl.when((role == 3) & crosses(piece))
+        @pl.when(((role == 3) & crosses(piece)) | ((role == 0) & crosses_back(piece)))
         def _():
             to_slot(slots.at[3, piece], 3, piece, 7, -3).wait_send()
+
+        @pl.when(role == 2)
+        def _():
+            to_relay(piece, 4).wait_send()
+
+        @pl.when(relayed(piece))
+        def _():
+            to_slot(relay.at[piece], 1, piece, 8, 4).wait_send()
 
         return 0
 
@@ -422,11 +482,12 @@
             pltpu.VMEM(piece, jnp.bfloat16),
             pltpu.VMEM(piece, jnp.bfloat16),
             pltpu.VMEM(piece, jnp.bfloat16),
+            pltpu.VMEM(piece, jnp.bfloat16),
             pltpu.VMEM((3, frame_count + past_frames.shape[0], padded, channels), jnp.bfloat16),
             pltpu.VMEM(conv_weight.shape, jnp.bfloat16),
             pltpu.VMEM((3, frame_count, padded + 16, channels), jnp.float32),
-            pltpu.SemaphoreType.DMA((6, PIECES)),
-            pltpu.SemaphoreType.DMA((8, PIECES)),
+            pltpu.SemaphoreType.DMA((7, PIECES)),
+            pltpu.SemaphoreType.DMA((9, PIECES)),
             pltpu.SemaphoreType.DMA((2,)),
             pltpu.SemaphoreType.DMA((2,)),
             pltpu.SemaphoreType.DMA,
@@ -448,8 +509,8 @@
         keys_values,
         frames,
         past_frames,
-        norm_gain.reshape(1, channels),
-        conv_bias.reshape(1, channels),
+        norm_gain,
+        conv_bias,
         conv_weight,
     )
 

time: 131 us -> 128 us (0.977); the launches traced: 129 us -> 128 us
  local copies, waits for them, and re-layouts: 8.55 us -> 6.04 us
    reshape x2 -> x0, local copies, waits for them, and re-layouts: 2.52 us -> none  [the longest x1 1.26 us: shards(): norm_gain.reshape(1, channels)]
where the time goes in v3:
time: 128 us
  Pallas kernels  121 us (95%)
  local copies, waits for them, and re-layouts  6.04 us (5%)
  between operations  1.29 us (1%)
    pallas_call x1, Pallas kernels, shards(): pl.pallas_call(functools.partial(block_kernel, n), out_shape=(jax.ShapeDt...  121 us
    unnamed x6, local copies, waits for them, and re-layouts  6.04 us

profile of v3, /device:TPU:0, one launch (start us, length us, event | category | flops | bytes accessed | tf_op | source)
XLA Modules:
  0.0 127.9 jit_solution(11751494805459274476)
XLA Ops:
  1.3 1.4 %copy.12.mask_ref = s32[16,3]{1,0:T(8,128)} copy(s32[16,3]{0,1:T(4,128)} %param.13) | data formatting | bytes 384 | tf_op args[3]
  2.6 1.5 %copy.13.past_ref = bf16[2,1,52,384]{3,2,1,0:T(8,128)(2,1)} copy(bf16[2,1,52,384]{3,0,2,1:T(2,128)(2,1)} %param.16) | data formatting | bytes 159744 | tf_op args[6]
  4.2 120.5 %spans_and_decoder.1 = (bf16[256,2560]{1,0:T(8,128)(2,1)}, bf16[3,1,52,384]{3,2,1,0:T(8,128)(2,1)}) custom-call(s32[1]{0:T(128)S(6)} %copy.16.owner_ref, s32[16,3]{1,0:T(8,128)} %copy.12.mask_ref, s32[16]{0:T(128)} %lengths_ref.1, bf16[256,2560]{1,0:T(8,128)(2,1)} %q_ref.1, bf16[2,256,2560]{2,1,0:T(8,128)(2,1)} %kv_ref.1, ...), custom_call_target="tpu_custom_call" | custom-call | flops 4597612544 | bytes 13205504 | tf_op jit(solution)/shard_map/spans_and_decoder/pallas_call | solution.py:471
  124.7 0.0 copy-start
  124.7 2.5 %copy.17 = bf16[256,2560]{1,0:T(8,128)(2,1)} copy(bf16[256,2560]{1,0:T(8,128)(2,1)} %get-tuple-element.4) | data formatting | bytes 2621440
  127.2 0.0 copy-done
  127.2 0.7 copy.18
Async XLA Ops:
  124.7 2.5 %copy-start = (bf16[3,1,52,384]{3,2,1,0:T(8,128)(2,1)S(1)}, bf16[3,1,52,384]{3,2,1,0:T(8,128)(2,1)}, u32[]{:S(2)}) copy-start(bf16[3,1,52,384]{3,2,1,0:T(8,128)(2,1)} %get-tuple-element.5) | copy-start | bytes 359428

commit v4 on v3

--- a/solution.py
+++ b/solution.py
@@ -9,8 +9,9 @@
 
 DH = 128
 WIN = 4
-PIECES = 10
+PIECES = 20
 AHEAD = 4
+HOP = 2
 LOG2E = 1.4426950408889634
 MESH = pl.DeviceIdType.MESH
 
@@ -156,23 +157,25 @@
                 for slot, lane, offset in copies:
                     to_slot(own(piece), slot, piece, lane, offset).start()
 
-    passed = {
-        0: ((1, 2, 2, 1), (0, 1, 3, 1)),
-        2: ((2, 0, 2, -2), (1, 2, 3, 1)),
-        3: ((1, 0, 2, -1),),
-    }
-    kept = {0: (2,), 1: (0, 1, 2), 2: (0,), 3: (0, 2)}
-
-    def window(piece):
-        pass_relayed(piece)
-        for which in range(4):
+    passed = {2: ((2, 0, 2, -2), (1, 2, 3, 1)), 3: ((1, 0, 2, -1),)}
+    passed_again = {0: ((1, 2, 2, 1), (0, 1, 3, 1))}
+    kept = {0: (2,), 2: (0,), 3: (0, 2)}
+
+    def pass_on(piece, table):
+        for which, copies in table.items():
 
             @pl.when(role == which)
             def _():
-                for slot, there, lane, offset in passed.get(which, ()):
+                for slot, there, lane, offset in copies:
                     arrived(slot, piece)
                     to_slot(slots.at[slot, piece], there, piece, lane, offset).start()
-                for slot in kept[which]:
+
+    def keep(piece):
+        for which, slots_here in kept.items():
+
+            @pl.when(role == which)
+            def _():
+                for slot in slots_here:
                     arrived(slot, piece)
 
     anchor = owner_ref[0]
@@ -309,7 +312,15 @@
 
         @pl.when(t < PIECES)
         def _():
-            window(t)
+            pass_on(t, passed)
+            pass_relayed(t)
+
+        known = t - 1
+
+        @pl.when(within(known))
+        def _():
+            pass_on(known, passed_again)
+            keep(known)
 
         @pl.when(t == 2)
         def _():
@@ -323,10 +334,11 @@
         def _():
             decode()
 
-        rising = t - z
-        falling = t - (rows - 1 - z)
-        final = t - (rows - 1)
-        ready = t - rows
+        rising = known - HOP * z
+        falling = known - HOP * (rows - 1 - z)
+        final = known - HOP * (rows - 1)
+        crossed = final - 1
+        ready = final - 2
 
         @pl.when(within(rising) & waves(rising))
         def _():
@@ -378,27 +390,32 @@
             def _():
                 to_slot(slots.at[3, final], 3, final, 6, 1).start()
 
+        @pl.when(within(crossed) & (role == 0) & crosses(crossed))
+        def _():
+            arrived(3, crossed)
+            to_slot(slots.at[3, crossed], 3, crossed, 6, 1).start()
+
+        @pl.when(within(crossed) & (role == 3) & crosses_back(crossed))
+        def _():
+            arrived(3, crossed)
+            to_slot(slots.at[3, crossed], 3, crossed, 6, -1).start()
+
         @pl.when(within(ready))
         def _():
-            @pl.when((role == 0) & crosses(ready))
+            @pl.when(role == 1)
+            def _():
+                for slot in range(3):
+                    arrived(slot, ready)
+
+            @pl.when((role == 1) | (role == 2))
             def _():
                 arrived(3, ready)
-                to_slot(slots.at[3, ready], 3, ready, 6, 1).start()
-
-            @pl.when((role == 3) & crosses_back(ready))
-            def _():
-                arrived(3, ready)
-                to_slot(slots.at[3, ready], 3, ready, 6, -1).start()
-
-            @pl.when((role == 1) | (role == 2))
-            def _():
-                arrived(3, ready)
 
             attend(ready)
 
         return 0
 
-    lax.fori_loop(0, PIECES + rows, step, 0)
+    lax.fori_loop(0, PIECES + 3 + HOP * (rows - 1), step, 0)
 
     def finish(piece, _):
         for which in range(4):
@@ -407,7 +424,7 @@
             def _():
                 for slot, lane, offset in direct[which]:
                     to_slot(own(piece), slot, piece, lane, offset).wait_send()
-                for slot, there, lane, offset in passed.get(which, ()):
+                for slot, there, lane, offset in passed.get(which, ()) + passed_again.get(which, ()):
                     to_slot(slots.at[slot, piece], there, piece, lane, offset).wait_send()
 
         @pl.when(waves(piece) & (z < rows - 1))

time: 128 us -> 112 us (0.88)
  Pallas kernels: 121 us -> 104 us
    pallas_call x1, Pallas kernels: 121 us -> 104 us  [shards(): pl.pallas_call(functools.partial(block_kernel, n), out_shape=(jax.ShapeDt...]
where the time goes in v4:
time: 112 us; the launch traced here: 111 us
  Pallas kernels  104 us (93%)
  local copies, waits for them, and re-layouts  6.04 us (5%)
  between operations  1.29 us (1%)
    pallas_call x1, Pallas kernels, shards(): pl.pallas_call(functools.partial(block_kernel, n), out_shape=(jax.ShapeDt...  104 us
    unnamed x6, local copies, waits for them, and re-layouts  6.04 us

profile of v4, /device:TPU:0, one launch (start us, length us, event | category | flops | bytes accessed | tf_op | source)
XLA Modules:
  0.0 111.3 jit_solution(15256808789920364295)
XLA Ops:
  1.3 1.4 %copy.12.mask_ref = s32[16,3]{1,0:T(8,128)} copy(s32[16,3]{0,1:T(4,128)} %param.13) | data formatting | bytes 384 | tf_op args[3]
  2.6 1.5 %copy.13.past_ref = bf16[2,1,52,384]{3,2,1,0:T(8,128)(2,1)} copy(bf16[2,1,52,384]{3,0,2,1:T(2,128)(2,1)} %param.16) | data formatting | bytes 159744 | tf_op args[6]
  4.2 104.0 %spans_and_decoder.1 = (bf16[256,2560]{1,0:T(8,128)(2,1)}, bf16[3,1,52,384]{3,2,1,0:T(8,128)(2,1)}) custom-call(s32[1]{0:T(128)S(6)} %copy.16.owner_ref, s32[16,3]{1,0:T(8,128)} %copy.12.mask_ref, s32[16]{0:T(128)} %lengths_ref.1, bf16[256,2560]{1,0:T(8,128)(2,1)} %q_ref.1, bf16[2,256,2560]{2,1,0:T(8,128)(2,1)} %kv_ref.1, ...), custom_call_target="tpu_custom_call" | custom-call | flops 4597612544 | bytes 13205504 | tf_op jit(solution)/shard_map/spans_and_decoder/pallas_call | solution.py:488
  108.1 0.0 copy-start
  108.2 2.5 %copy.17 = bf16[256,2560]{1,0:T(8,128)(2,1)} copy(bf16[256,2560]{1,0:T(8,128)(2,1)} %get-tuple-element.4) | data formatting | bytes 2621440
  110.6 0.0 copy-done
  110.7 0.7 copy.18
Async XLA Ops:
  108.1 2.5 %copy-start = (bf16[3,1,52,384]{3,2,1,0:T(8,128)(2,1)S(1)}, bf16[3,1,52,384]{3,2,1,0:T(8,128)(2,1)}, u32[]{:S(2)}) copy-start(bf16[3,1,52,384]{3,2,1,0:T(8,128)(2,1)} %get-tuple-element.5) | copy-start | bytes 359428

commit v5 on v4

--- a/solution.py
+++ b/solution.py
@@ -12,6 +12,7 @@
 PIECES = 20
 AHEAD = 4
 HOP = 2
+LAG = 2
 LOG2E = 1.4426950408889634
 MESH = pl.DeviceIdType.MESH
 
@@ -30,6 +31,7 @@
     weight_ref,
     out_ref,
     decoded_ref,
+    limit_ref,
     slots,
     relay,
     up_in,
@@ -47,7 +49,7 @@
 ):
     tokens = q_ref.shape[0]
     frames, _, cols, channels = frames_ref.shape
-    past = past_ref.shape[0]
+    past = past_ref.shape[2]
     padded = taps.shape[2]
     rows = n // 4
     width = q_ref.shape[1] // PIECES
@@ -202,9 +204,10 @@
 
     position = lax.rem(me - anchor - 1 + 2 * n, n)
     length = lengths_ref[me]
+    limit_ref[...] = jnp.full(limit_ref.shape, length, jnp.int32)
     limits = [length]
     for offset in range(1, WIN):
-        allowed = (position >= offset) & (mask_ref[position, offset - 1] == 1)
+        allowed = (position >= offset) & (mask_ref[offset - 1, position] == 1)
         limits.append(jnp.where(allowed, lengths_ref[at(-offset)], 0))
     limits.append(jnp.where(behind == 0, 0, lengths_ref[anchor]))
 
@@ -212,7 +215,7 @@
         spare = partial.at[0, 0, 0:padded, :]
         for frame in range(past + frames):
             if frame < past:
-                value = past_ref[frame, 0].astype(jnp.float32)
+                value = past_ref[0].astype(jnp.float32)[:, frame, :]
             else:
                 value = frames_ref[frame - past, 0].astype(jnp.float32)
                 squares = jnp.mean(value * value, axis=-1, keepdims=True)
@@ -273,7 +276,6 @@
     def attend(piece):
         token = lax.broadcasted_iota(jnp.int32, (1, tokens), 1)
         hidden = [jnp.where(token < limit, 0.0, -1e30) for limit in limits]
-        row = lax.broadcasted_iota(jnp.int32, (tokens, 1), 0)
         for sub in range(width // DH):
             cols = pl.ds(pl.multiple_of(piece * width + sub * DH, DH), DH)
             inner = slice(sub * DH, (sub + 1) * DH)
@@ -296,7 +298,7 @@
                     weights[block].astype(jnp.bfloat16), value, preferred_element_type=jnp.float32
                 )
                 blended = term if blended is None else blended + term
-            out_ref[:, cols] = jnp.where(row < length, blended / total, 0.0).astype(out_ref.dtype)
+            out_ref[:, cols] = (blended / total).astype(out_ref.dtype)
 
     def start(piece, _):
         send_own(piece)
@@ -315,7 +317,7 @@
             pass_on(t, passed)
             pass_relayed(t)
 
-        known = t - 1
+        known = t - LAG
 
         @pl.when(within(known))
         def _():
@@ -337,8 +339,8 @@
         rising = known - HOP * z
         falling = known - HOP * (rows - 1 - z)
         final = known - HOP * (rows - 1)
-        crossed = final - 1
-        ready = final - 2
+        crossed = final - LAG
+        ready = crossed - 1
 
         @pl.when(within(rising) & waves(rising))
         def _():
@@ -415,7 +417,7 @@
 
         return 0
 
-    lax.fori_loop(0, PIECES + 3 + HOP * (rows - 1), step, 0)
+    lax.fori_loop(0, PIECES + 2 * LAG + 1 + HOP * (rows - 1), step, 0)
 
     def finish(piece, _):
         for which in range(4):
@@ -485,14 +487,15 @@
     conv_flops = 2 * frame_count * frame_cols * conv_weight.size
     scalars = pl.BlockSpec(memory_space=pltpu.SMEM)
     whole = pl.BlockSpec(memory_space=pltpu.VMEM)
-    return pl.pallas_call(
+    attended, decoded, limit = pl.pallas_call(
         functools.partial(block_kernel, n),
         out_shape=(
             jax.ShapeDtypeStruct((rows, cols), jnp.bfloat16),
             jax.ShapeDtypeStruct(frames.shape, jnp.bfloat16),
+            jax.ShapeDtypeStruct((8, 128), jnp.int32),
         ),
         in_specs=[scalars] * 3 + [whole] * 6 + [pl.BlockSpec(memory_space=pl.ANY)],
-        out_specs=(whole, whole),
+        out_specs=(whole, whole, whole),
         scratch_shapes=[
             pltpu.VMEM((4,) + piece, jnp.bfloat16),
             pltpu.VMEM(piece, jnp.bfloat16),
@@ -520,16 +523,18 @@
         name="spans_and_decoder",
     )(
         owner,
-        span_mask,
+        span_mask.T,
         lengths,
         queries,
         keys_values,
         frames,
-        past_frames,
+        jnp.transpose(past_frames, (1, 2, 0, 3)),
         norm_gain,
         conv_bias,
         conv_weight,
     )
+    row_ids = lax.broadcasted_iota(jnp.int32, (rows, 1), 0)
+    return jnp.where(row_ids < limit[:1, :1], attended, 0.0).astype(jnp.bfloat16), decoded
 
 
 def solution(mesh):

time: 112 us -> 107 us (0.955)
  local copies, waits for them, and re-layouts: 6.04 us -> 1.85 us
  Pallas kernels: 104 us -> 100 us
  other arithmetic: 0 us -> 3.21 us
    unnamed x6 -> x3, local copies, waits for them, and re-layouts: 6.04 us -> 0.65 us
    pallas_call x1, Pallas kernels: 104 us -> 100 us  [shards(): pl.pallas_call(functools.partial(block_kernel, n), out_shape=(jax.ShapeDt...]
    select_n x0 -> x1, other arithmetic: none -> 2.56 us  [shards(): jnp.where(row_ids < limit[:1, :1], attended, 0.0).astype(jnp.bfloat16)]
    slice x0 -> x1, local copies, waits for them, and re-layouts: none -> 1.19 us  [shards(): limit[:1, :1]]
where the time goes in v5:
time: 107 us
  Pallas kernels  100 us (93%)
  other arithmetic  3.21 us (3%)
  local copies, waits for them, and re-layouts  1.85 us (2%)
  between operations  1.3 us (1%)
    pallas_call x1, Pallas kernels, shards(): pl.pallas_call(functools.partial(block_kernel, n), out_shape=(jax.ShapeDt...  100 us
    select_n x1, other arithmetic, shards(): jnp.where(row_ids < limit[:1, :1], attended, 0.0).astype(jnp.bfloat16)  2.56 us

profile of v5, /device:TPU:0, one launch (start us, length us, event | category | flops | bytes accessed | tf_op | source)
XLA Modules:
  0.0 106.8 jit_solution(2965439962158836081)
XLA Ops:
  1.3 100.4 %spans_and_decoder.1 = (bf16[256,2560]{1,0:T(8,128)(2,1)}, bf16[3,1,52,384]{3,2,1,0:T(8,128)(2,1)}, s32[8,128]{1,0:T(8,128)}) custom-call(s32[1]{0:T(128)S(6)} %copy.13.owner_ref, s32[3,16]{1,0:T(4,128)} %bitcast.4, s32[16]{0:T(128)} %lengths_ref.1, bf16[256,2560]{1,0:T(8,128)(2,1)} %q_ref.1, bf16[2,256,2560]{2,1,0:T(8,128)(2,1)} %kv_ref.1, ...), custom_call_target="tpu_custom_call" | custom-call | flops 4597612544 | bytes 13205504 | tf_op jit(solution)/shard_map/spans_and_decoder/pallas_call | solution.py:490
  101.7 1.2 %slice.3 = s32[1,1]{1,0:T(1,128)} slice(s32[8,128]{1,0:T(8,128)} %get-tuple-element.5), slice={[0:1], [0:1]} | slice | bytes 8 | tf_op jit(solution)/shard_map/slice | solution.py:537
  102.9 0.6 iota_compare_fusion
  103.5 0.0 copy-start
  103.5 2.6 %broadcast_select_fusion = bf16[256,2560]{1,0:T(8,128)(2,1)} fusion(bf16[256,2560]{1,0:T(8,128)(2,1)} %get-tuple-element.6, pred[256]{0:T(512)(128)(4,1)S(1)} %iota_compare_fusion), kind=kLoop, calls=%fused_computation | loop fusion | flops 655360 | bytes 2621696 | tf_op jit(solution)/shard_map/jit(_where)/select_n | solution.py:537
  106.1 0.0 copy-done
  106.1 0.7 copy.14
Async XLA Ops:
  103.5 2.6 %copy-start = (bf16[3,1,52,384]{3,2,1,0:T(8,128)(2,1)S(1)}, bf16[3,1,52,384]{3,2,1,0:T(8,128)(2,1)}, u32[]{:S(2)}) copy-start(bf16[3,1,52,384]{3,2,1,0:T(8,128)(2,1)} %get-tuple-element.11) | copy-start | bytes 359428

commit v6 on v5

--- a/solution.py
+++ b/solution.py
@@ -31,9 +31,11 @@
     weight_ref,
     out_ref,
     decoded_ref,
-    limit_ref,
     slots,
     relay,
+    sums,
+    tops,
+    totals,
     up_in,
     down_in,
     up_out,
@@ -204,7 +206,6 @@
 
     position = lax.rem(me - anchor - 1 + 2 * n, n)
     length = lengths_ref[me]
-    limit_ref[...] = jnp.full(limit_ref.shape, length, jnp.int32)
     limits = [length]
     for offset in range(1, WIN):
         allowed = (position >= offset) & (mask_ref[offset - 1, position] == 1)
@@ -273,32 +274,39 @@
                 total = total + partial[col_tap, frame, 7 + col_tap : 7 + col_tap + cols, :]
             decoded_ref[frame, 0] = total.astype(decoded_ref.dtype)
 
-    def attend(piece):
-        token = lax.broadcasted_iota(jnp.int32, (1, tokens), 1)
-        hidden = [jnp.where(token < limit, 0.0, -1e30) for limit in limits]
-        for sub in range(width // DH):
-            cols = pl.ds(pl.multiple_of(piece * width + sub * DH, DH), DH)
-            inner = slice(sub * DH, (sub + 1) * DH)
-            query = q_ref[:, cols]
-            scores = []
-            for block in range(5):
-                key = kv_ref[0, :, cols] if block == 0 else slots[block - 1, piece, 0, :, inner]
-                score = lax.dot_general(
-                    query, key, (((1,), (1,)), ((), ())), preferred_element_type=jnp.float32
-                )
-                scores.append(score * (DH**-0.5 * LOG2E) + hidden[block])
-            top = functools.reduce(jnp.maximum, scores)
-            top = jnp.max(top, axis=-1, keepdims=True)
-            weights = [jnp.exp2(score - top) for score in scores]
-            total = jnp.sum(functools.reduce(jnp.add, weights), axis=-1, keepdims=True)
-            blended = None
-            for block in range(5):
-                value = kv_ref[1, :, cols] if block == 0 else slots[block - 1, piece, 1, :, inner]
-                term = jnp.dot(
-                    weights[block].astype(jnp.bfloat16), value, preferred_element_type=jnp.float32
-                )
-                blended = term if blended is None else blended + term
-            out_ref[:, cols] = (blended / total).astype(out_ref.dtype)
+    token = lax.broadcasted_iota(jnp.int32, (1, tokens), 1)
+    row = lax.broadcasted_iota(jnp.int32, (tokens, 1), 0)
+
+    def scores_of(piece, key, limit):
+        score = lax.dot_general(
+            q_ref[:, columns(piece)], key, (((1,), (1,)), ((), ())), preferred_element_type=jnp.float32
+        )
+        return score * (DH**-0.5 * LOG2E) + jnp.where(token < limit, 0.0, -1e30)
+
+    def blend(weights, value):
+        return jnp.dot(weights.astype(jnp.bfloat16), value, preferred_element_type=jnp.float32)
+
+    def attend_window(piece):
+        keys = [kv_ref[0, :, columns(piece)]] + [slots[slot, piece, 0] for slot in range(WIN - 1)]
+        values = [kv_ref[1, :, columns(piece)]] + [slots[slot, piece, 1] for slot in range(WIN - 1)]
+        scores = [scores_of(piece, key, limit) for key, limit in zip(keys, limits)]
+        top = jnp.max(functools.reduce(jnp.maximum, scores), axis=-1, keepdims=True)
+        weights = [jnp.exp2(score - top) for score in scores]
+        total = jnp.sum(functools.reduce(jnp.add, weights), axis=-1, keepdims=True)
+        blended = [blend(weight, value) for weight, value in zip(weights, values)]
+        sums[piece] = functools.reduce(jnp.add, blended)
+        tops[piece] = jnp.broadcast_to(top, tops.shape[1:])
+        totals[piece] = jnp.broadcast_to(total, totals.shape[1:])
+
+    def attend_anchor(piece):
+        score = scores_of(piece, slots[3, piece, 0], limits[WIN])
+        before = tops[piece]
+        top = jnp.maximum(before, jnp.max(score, axis=-1, keepdims=True))
+        weights = jnp.exp2(score - top[:, :1])
+        scale = jnp.exp2(before - top)
+        total = totals[piece] * scale + jnp.sum(weights, axis=-1, keepdims=True)
+        blended = (sums[piece] * scale + blend(weights, slots[3, piece, 1])) / total
+        out_ref[:, columns(piece)] = jnp.where(row < length, blended, 0.0).astype(out_ref.dtype)
 
     def start(piece, _):
         send_own(piece)
@@ -402,18 +410,22 @@
             arrived(3, crossed)
             to_slot(slots.at[3, crossed], 3, crossed, 6, -1).start()
 
+        @pl.when(within(known - 1))
+        def _():
+            @pl.when(role == 1)
+            def _():
+                for slot in range(3):
+                    arrived(slot, known - 1)
+
+            attend_window(known - 1)
+
         @pl.when(within(ready))
         def _():
-            @pl.when(role == 1)
-            def _():
-                for slot in range(3):
-                    arrived(slot, ready)
-
             @pl.when((role == 1) | (role == 2))
             def _():
                 arrived(3, ready)
 
-            attend(ready)
+            attend_anchor(ready)
 
         return 0
 
@@ -487,18 +499,20 @@
     conv_flops = 2 * frame_count * frame_cols * conv_weight.size
     scalars = pl.BlockSpec(memory_space=pltpu.SMEM)
     whole = pl.BlockSpec(memory_space=pltpu.VMEM)
-    attended, decoded, limit = pl.pallas_call(
+    return pl.pallas_call(
         functools.partial(block_kernel, n),
         out_shape=(
             jax.ShapeDtypeStruct((rows, cols), jnp.bfloat16),
             jax.ShapeDtypeStruct(frames.shape, jnp.bfloat16),
-            jax.ShapeDtypeStruct((8, 128), jnp.int32),
         ),
         in_specs=[scalars] * 3 + [whole] * 6 + [pl.BlockSpec(memory_space=pl.ANY)],
-        out_specs=(whole, whole, whole),
+        out_specs=(whole, whole),
         scratch_shapes=[
             pltpu.VMEM((4,) + piece, jnp.bfloat16),
             pltpu.VMEM(piece, jnp.bfloat16),
+            pltpu.VMEM((PIECES, rows, DH), jnp.float32),
+            pltpu.VMEM((PIECES, rows, DH), jnp.float32),
+            pltpu.VMEM((PIECES, rows, DH), jnp.float32),
             pltpu.VMEM(piece, jnp.bfloat16),
             pltpu.VMEM(piece, jnp.bfloat16),
             pltpu.VMEM(piece, jnp.bfloat16),
@@ -533,8 +547,6 @@
         conv_bias,
         conv_weight,
     )
-    row_ids = lax.broadcasted_iota(jnp.int32, (rows, 1), 0)
-    return jnp.where(row_ids < limit[:1, :1], attended, 0.0).astype(jnp.bfloat16), decoded
 
 
 def solution(mesh):

time: 107 us -> 106 us (level)
  other arithmetic: 3.21 us -> 0 us
  local copies, waits for them, and re-layouts: 1.85 us -> 3.15 us
    select_n x1 -> x0, other arithmetic: 2.56 us -> none  [shards(): jnp.where(row_ids < limit[:1, :1], attended, 0.0).astype(jnp.bfloat16)]
    unnamed x3 -> x4, local copies, waits for them, and re-layouts: 0.65 us -> 3.15 us
    slice x1 -> x0, local copies, waits for them, and re-layouts: 1.19 us -> none  [shards(): limit[:1, :1]]
where the time goes in v6:
time: 106 us
  Pallas kernels  101 us (95%)
  local copies, waits for them, and re-layouts  3.15 us (3%)
  between operations  1.3 us (1%)
    pallas_call x1, Pallas kernels, shards(): pl.pallas_call(functools.partial(block_kernel, n), out_shape=(jax.ShapeDt...  101 us
    unnamed x4, local copies, waits for them, and re-layouts  3.15 us

profile of v6, /device:TPU:0, one launch (start us, length us, event | category | flops | bytes accessed | tf_op | source)
XLA Modules:
  0.0 105.5 jit_solution(184212092730259672)
XLA Ops:
  1.3 101.1 %spans_and_decoder.1 = (bf16[256,2560]{1,0:T(8,128)(2,1)}, bf16[3,1,52,384]{3,2,1,0:T(8,128)(2,1)}) custom-call(s32[1]{0:T(128)S(6)} %copy.14.owner_ref, s32[3,16]{1,0:T(4,128)} %bitcast.3, s32[16]{0:T(128)} %lengths_ref.1, bf16[256,2560]{1,0:T(8,128)(2,1)} %q_ref.1, bf16[2,256,2560]{2,1,0:T(8,128)(2,1)} %kv_ref.1, bf16[3,1,52,384]{3,2,1,0:T(8,128)(2,1)} %frames_ref.1, ...), custom_call_target="tpu_custom_call" | custom-call | flops 4597612544 | bytes 13205504 | tf_op jit(solution)/shard_map/spans_and_decoder/pallas_call | solution.py:502
  102.4 0.0 copy-start
  102.4 2.5 %copy.15 = bf16[256,2560]{1,0:T(8,128)(2,1)} copy(bf16[256,2560]{1,0:T(8,128)(2,1)} %get-tuple-element.4) | data formatting | bytes 2621440
  104.9 0.0 copy-done
  104.9 0.7 copy.16
Async XLA Ops:
  102.4 2.5 %copy-start = (bf16[3,1,52,384]{3,2,1,0:T(8,128)(2,1)S(1)}, bf16[3,1,52,384]{3,2,1,0:T(8,128)(2,1)}, u32[]{:S(2)}) copy-start(bf16[3,1,52,384]{3,2,1,0:T(8,128)(2,1)} %get-tuple-element.5) | copy-start | bytes 359428

commit v7 on v6

--- a/solution.py
+++ b/solution.py
@@ -184,7 +184,7 @@
 
     anchor = owner_ref[0]
     behind = lax.rem(me - anchor + n, n)
-    group = jnp.where(role == 0, lax.rem((anchor + 3) // 4, rows), anchor // 4)
+    group = jnp.where(role == 1, lax.rem((anchor + 2) // 4, rows), anchor // 4)
 
     def mine(piece, part):
         value = jnp.where(behind == 2, slots[1, piece, part], slots[2, piece, part])
@@ -199,7 +199,7 @@
 
     def waves(piece):
         upper = (role == 3) & jnp.logical_not(crosses_back(piece))
-        return upper | ((role == 0) & jnp.logical_not(crosses(piece)))
+        return upper | ((role == 1) & jnp.logical_not(crosses(piece)))
 
     def within(piece):
         return (piece >= 0) & (piece < PIECES)
@@ -344,9 +344,16 @@
         def _():
             decode()
 
-        rising = known - HOP * z
-        falling = known - HOP * (rows - 1 - z)
-        final = known - HOP * (rows - 1)
+        settled = known - 1
+
+        @pl.when(within(settled) & (role == 1))
+        def _():
+            for slot in range(3):
+                arrived(slot, settled)
+
+        rising = settled - HOP * z
+        falling = settled - HOP * (rows - 1 - z)
+        final = settled - HOP * (rows - 1)
         crossed = final - LAG
         ready = crossed - 1
 
@@ -386,42 +393,28 @@
 
             @pl.when((role == 3) & crosses(final))
             def _():
-                to_slot(slots.at[3, final], 3, final, 7, -3).start()
-
-            @pl.when((role == 0) & crosses_back(final))
-            def _():
-                to_slot(slots.at[3, final], 3, final, 7, 3).start()
-
-            @pl.when(role == 3)
-            def _():
-                to_slot(slots.at[3, final], 3, final, 6, -1).start()
-
-            @pl.when(role == 0)
-            def _():
-                to_slot(slots.at[3, final], 3, final, 6, 1).start()
-
-        @pl.when(within(crossed) & (role == 0) & crosses(crossed))
-        def _():
-            arrived(3, crossed)
-            to_slot(slots.at[3, crossed], 3, crossed, 6, 1).start()
-
-        @pl.when(within(crossed) & (role == 3) & crosses_back(crossed))
-        def _():
-            arrived(3, crossed)
-            to_slot(slots.at[3, crossed], 3, crossed, 6, -1).start()
-
-        @pl.when(within(known - 1))
-        def _():
-            @pl.when(role == 1)
-            def _():
-                for slot in range(3):
-                    arrived(slot, known - 1)
-
-            attend_window(known - 1)
+                to_slot(slots.at[3, final], 3, final, 7, -2).start()
+
+            @pl.when((role == 1) & crosses_back(final))
+            def _():
+                to_slot(slots.at[3, final], 3, final, 7, 2).start()
+
+            to_slot(slots.at[3, final], 3, final, 6, -1).start()
+
+        @pl.when(within(crossed))
+        def _():
+            @pl.when(((role == 1) & crosses(crossed)) | ((role == 3) & crosses_back(crossed)))
+            def _():
+                arrived(3, crossed)
+                to_slot(slots.at[3, crossed], 3, crossed, 6, -1).start()
+
+        @pl.when(within(settled))
+        def _():
+            attend_window(settled)
 
         @pl.when(within(ready))
         def _():
-            @pl.when((role == 1) | (role == 2))
+            @pl.when((role == 0) | (role == 2))
             def _():
                 arrived(3, ready)
 
@@ -429,7 +422,7 @@
 
         return 0
 
-    lax.fori_loop(0, PIECES + 2 * LAG + 1 + HOP * (rows - 1), step, 0)
+    lax.fori_loop(0, PIECES + 2 * LAG + 2 + HOP * (rows - 1), step, 0)
 
     def finish(piece, _):
         for which in range(4):
@@ -449,11 +442,11 @@
         def _():
             wave(down_out, down_in, 5, piece, -4).wait_send()
 
-        @pl.when((role == 0) | (role == 3))
-        def _():
-            to_slot(slots.at[3, piece], 3, piece, 6, 1).wait_send()
-
-        @pl.when(((role == 3) & crosses(piece)) | ((role == 0) & crosses_back(piece)))
+        @pl.when((role == 1) | (role == 3))
+        def _():
+            to_slot(slots.at[3, piece], 3, piece, 6, -1).wait_send()
+
+        @pl.when(((role == 3) & crosses(piece)) | ((role == 1) & crosses_back(piece)))
         def _():
             to_slot(slots.at[3, piece], 3, piece, 7, -3).wait_send()
 

time: 106 us -> 104 us (0.981)
  Pallas kernels: 101 us -> 99.2 us
    pallas_call x1, Pallas kernels: 101 us -> 99.2 us  [shards(): pl.pallas_call(functools.partial(block_kernel, n), out_shape=(jax.ShapeDt...]
where the time goes in v7:
time: 104 us
  Pallas kernels  99.2 us (95%)
  local copies, waits for them, and re-layouts  3.15 us (3%)
  between operations  1.3 us (1%)
    pallas_call x1, Pallas kernels, shards(): pl.pallas_call(functools.partial(block_kernel, n), out_shape=(jax.ShapeDt...  99.2 us
    unnamed x4, local copies, waits for them, and re-layouts  3.15 us

profile of v7, /device:TPU:0, one launch (start us, length us, event | category | flops | bytes accessed | tf_op | source)
XLA Modules:
  0.0 103.6 jit_solution(9608637812951724167)
XLA Ops:
  1.3 99.2 %spans_and_decoder.1 = (bf16[256,2560]{1,0:T(8,128)(2,1)}, bf16[3,1,52,384]{3,2,1,0:T(8,128)(2,1)}) custom-call(s32[1]{0:T(128)S(6)} %copy.14.owner_ref, s32[3,16]{1,0:T(4,128)} %bitcast.3, s32[16]{0:T(128)} %lengths_ref.1, bf16[256,2560]{1,0:T(8,128)(2,1)} %q_ref.1, bf16[2,256,2560]{2,1,0:T(8,128)(2,1)} %kv_ref.1, bf16[3,1,52,384]{3,2,1,0:T(8,128)(2,1)} %frames_ref.1, ...), custom_call_target="tpu_custom_call" | custom-call | flops 4597612544 | bytes 13205504 | tf_op jit(solution)/shard_map/spans_and_decoder/pallas_call | solution.py:495
  100.5 0.0 copy-start
  100.5 2.5 %copy.15 = bf16[256,2560]{1,0:T(8,128)(2,1)} copy(bf16[256,2560]{1,0:T(8,128)(2,1)} %get-tuple-element.4) | data formatting | bytes 2621440
  103.0 0.0 copy-done
  103.0 0.7 copy.16
Async XLA Ops:
  100.5 2.5 %copy-start = (bf16[3,1,52,384]{3,2,1,0:T(8,128)(2,1)S(1)}, bf16[3,1,52,384]{3,2,1,0:T(8,128)(2,1)}, u32[]{:S(2)}) copy-start(bf16[3,1,52,384]{3,2,1,0:T(8,128)(2,1)} %get-tuple-element.5) | copy-start | bytes 359428

commit v8 on v7

--- a/solution.py
+++ b/solution.py
@@ -284,29 +284,38 @@
         return score * (DH**-0.5 * LOG2E) + jnp.where(token < limit, 0.0, -1e30)
 
     def blend(weights, value):
-        return jnp.dot(weights.astype(jnp.bfloat16), value, preferred_element_type=jnp.float32)
-
-    def attend_window(piece):
-        keys = [kv_ref[0, :, columns(piece)]] + [slots[slot, piece, 0] for slot in range(WIN - 1)]
-        values = [kv_ref[1, :, columns(piece)]] + [slots[slot, piece, 1] for slot in range(WIN - 1)]
-        scores = [scores_of(piece, key, limit) for key, limit in zip(keys, limits)]
-        top = jnp.max(functools.reduce(jnp.maximum, scores), axis=-1, keepdims=True)
-        weights = [jnp.exp2(score - top) for score in scores]
-        total = jnp.sum(functools.reduce(jnp.add, weights), axis=-1, keepdims=True)
-        blended = [blend(weight, value) for weight, value in zip(weights, values)]
-        sums[piece] = functools.reduce(jnp.add, blended)
-        tops[piece] = jnp.broadcast_to(top, tops.shape[1:])
-        totals[piece] = jnp.broadcast_to(total, totals.shape[1:])
-
-    def attend_anchor(piece):
-        score = scores_of(piece, slots[3, piece, 0], limits[WIN])
-        before = tops[piece]
-        top = jnp.maximum(before, jnp.max(score, axis=-1, keepdims=True))
-        weights = jnp.exp2(score - top[:, :1])
-        scale = jnp.exp2(before - top)
-        total = totals[piece] * scale + jnp.sum(weights, axis=-1, keepdims=True)
-        blended = (sums[piece] * scale + blend(weights, slots[3, piece, 1])) / total
-        out_ref[:, columns(piece)] = jnp.where(row < length, blended, 0.0).astype(out_ref.dtype)
+        wide = jnp.concatenate([value, jnp.ones_like(value)], axis=1)
+        return jnp.dot(weights.astype(jnp.bfloat16), wide, preferred_element_type=jnp.float32)
+
+    def attend_window(pieces):
+        scores = []
+        for piece in pieces:
+            keys = [kv_ref[0, :, columns(piece)]] + [slots[slot, piece, 0] for slot in range(WIN - 1)]
+            scores.append([scores_of(piece, key, limit) for key, limit in zip(keys, limits)])
+        for which, piece in enumerate(pieces):
+            values = [kv_ref[1, :, columns(piece)]] + [slots[slot, piece, 1] for slot in range(WIN - 1)]
+            top = jnp.max(functools.reduce(jnp.maximum, scores[which]), axis=-1, keepdims=True)
+            blended = [
+                blend(jnp.exp2(score - top), value) for score, value in zip(scores[which], values)
+            ]
+            blended = functools.reduce(jnp.add, blended)
+            sums[piece] = blended[:, :DH]
+            totals[piece] = blended[:, DH:]
+            tops[piece] = jnp.broadcast_to(top, tops.shape[1:])
+
+    def attend_anchor(pieces):
+        scores = [scores_of(piece, slots[3, piece, 0], limits[WIN]) for piece in pieces]
+        for score, piece in zip(scores, pieces):
+            before = tops[piece]
+            top = jnp.maximum(before, jnp.max(score, axis=-1, keepdims=True))
+            added = blend(jnp.exp2(score - top[:, :1]), slots[3, piece, 1])
+            scale = jnp.exp2(before - top)
+            total = totals[piece] * scale + added[:, DH:]
+            blended = (sums[piece] * scale + added[:, :DH]) / total
+            out_ref[:, columns(piece)] = jnp.where(row < length, blended, 0.0).astype(out_ref.dtype)
+
+    def pair_ends(piece):
+        return within(piece) & (lax.rem(piece, 2) == 1)
 
     def start(piece, _):
         send_own(piece)
@@ -408,17 +417,18 @@
                 arrived(3, crossed)
                 to_slot(slots.at[3, crossed], 3, crossed, 6, -1).start()
 
-        @pl.when(within(settled))
-        def _():
-            attend_window(settled)
-
-        @pl.when(within(ready))
+        @pl.when(pair_ends(settled))
+        def _():
+            attend_window((settled - 1, settled))
+
+        @pl.when(pair_ends(ready))
         def _():
             @pl.when((role == 0) | (role == 2))
             def _():
+                arrived(3, ready - 1)
                 arrived(3, ready)
 
-            attend_anchor(ready)
+            attend_anchor((ready - 1, ready))
 
         return 0
 

time: 104 us -> 103 us (level)
  no operation moved by 1% of the time
where the time goes in v8:
time: 103 us
  Pallas kernels  98.4 us (96%)
  local copies, waits for them, and re-layouts  3.15 us (3%)
  between operations  1.3 us (1%)
    pallas_call x1, Pallas kernels, shards(): pl.pallas_call(functools.partial(block_kernel, n), out_shape=(jax.ShapeDt...  98.4 us
    unnamed x4, local copies, waits for them, and re-layouts  3.15 us

profile of v8, /device:TPU:0, one launch (start us, length us, event | category | flops | bytes accessed | tf_op | source)
XLA Modules:
  0.0 102.8 jit_solution(7875006421494758409)
XLA Ops:
  1.3 98.4 %spans_and_decoder.1 = (bf16[256,2560]{1,0:T(8,128)(2,1)}, bf16[3,1,52,384]{3,2,1,0:T(8,128)(2,1)}) custom-call(s32[1]{0:T(128)S(6)} %copy.14.owner_ref, s32[3,16]{1,0:T(4,128)} %bitcast.3, s32[16]{0:T(128)} %lengths_ref.1, bf16[256,2560]{1,0:T(8,128)(2,1)} %q_ref.1, bf16[2,256,2560]{2,1,0:T(8,128)(2,1)} %kv_ref.1, bf16[3,1,52,384]{3,2,1,0:T(8,128)(2,1)} %frames_ref.1, ...), custom_call_target="tpu_custom_call" | custom-call | flops 4597612544 | bytes 13205504 | tf_op jit(solution)/shard_map/spans_and_decoder/pallas_call | solution.py:505
  99.7 0.0 copy-start
  99.7 2.5 %copy.15 = bf16[256,2560]{1,0:T(8,128)(2,1)} copy(bf16[256,2560]{1,0:T(8,128)(2,1)} %get-tuple-element.4) | data formatting | bytes 2621440
  102.2 0.0 copy-done
  102.2 0.7 copy.16
Async XLA Ops:
  99.7 2.5 %copy-start = (bf16[3,1,52,384]{3,2,1,0:T(8,128)(2,1)S(1)}, bf16[3,1,52,384]{3,2,1,0:T(8,128)(2,1)}, u32[]{:S(2)}) copy-start(bf16[3,1,52,384]{3,2,1,0:T(8,128)(2,1)} %get-tuple-element.5) | copy-start | bytes 359428

commit v9 on v8

--- a/solution.py
+++ b/solution.py
@@ -191,15 +191,7 @@
         value = jnp.where(behind == 1, slots[0, piece, part], value)
         return jnp.where(behind == 0, kv_ref[part, :, columns(piece)], value)
 
-    def crosses(piece):
-        return lax.rem(piece, 5) == 1
-
-    def crosses_back(piece):
-        return lax.rem(piece, 5) == 3
-
-    def waves(piece):
-        upper = (role == 3) & jnp.logical_not(crosses_back(piece))
-        return upper | ((role == 1) & jnp.logical_not(crosses(piece)))
+    waves = lax.rem(role, 2) == 1
 
     def within(piece):
         return (piece >= 0) & (piece < PIECES)
@@ -363,10 +355,9 @@
         rising = settled - HOP * z
         falling = settled - HOP * (rows - 1 - z)
         final = settled - HOP * (rows - 1)
-        crossed = final - LAG
-        ready = crossed - 1
-
-        @pl.when(within(rising) & waves(rising))
+        ready = final - 1
+
+        @pl.when(within(rising) & waves)
         def _():
             @pl.when(z > 0)
             def _():
@@ -380,7 +371,7 @@
                     )
                 wave(up_out, up_in, 4, rising, 4).start()
 
-        @pl.when(within(falling) & waves(falling))
+        @pl.when(within(falling) & waves)
         def _():
             @pl.when(z < rows - 1)
             def _():
@@ -394,28 +385,13 @@
                     )
                 wave(down_out, down_in, 5, falling, -4).start()
 
-        @pl.when(within(final) & waves(final))
+        @pl.when(within(final) & waves)
         def _():
             for part in range(2):
                 value = jnp.where(group < z, up_in[final, part], down_in[final, part])
                 slots[3, final, part] = jnp.where(group == z, mine(final, part), value)
 
-            @pl.when((role == 3) & crosses(final))
-            def _():
-                to_slot(slots.at[3, final], 3, final, 7, -2).start()
-
-            @pl.when((role == 1) & crosses_back(final))
-            def _():
-                to_slot(slots.at[3, final], 3, final, 7, 2).start()
-
             to_slot(slots.at[3, final], 3, final, 6, -1).start()
-
-        @pl.when(within(crossed))
-        def _():
-            @pl.when(((role == 1) & crosses(crossed)) | ((role == 3) & crosses_back(crossed)))
-            def _():
-                arrived(3, crossed)
-                to_slot(slots.at[3, crossed], 3, crossed, 6, -1).start()
 
         @pl.when(pair_ends(settled))
         def _():
@@ -432,7 +408,7 @@
 
         return 0
 
-    lax.fori_loop(0, PIECES + 2 * LAG + 2 + HOP * (rows - 1), step, 0)
+    lax.fori_loop(0, PIECES + LAG + 2 + HOP * (rows - 1), step, 0)
 
     def finish(piece, _):
         for which in range(4):
@@ -444,21 +420,17 @@
                 for slot, there, lane, offset in passed.get(which, ()) + passed_again.get(which, ()):
                     to_slot(slots.at[slot, piece], there, piece, lane, offset).wait_send()
 
-        @pl.when(waves(piece) & (z < rows - 1))
+        @pl.when(waves & (z < rows - 1))
         def _():
             wave(up_out, up_in, 4, piece, 4).wait_send()
 
-        @pl.when(waves(piece) & (z > 0))
+        @pl.when(waves & (z > 0))
         def _():
             wave(down_out, down_in, 5, piece, -4).wait_send()
 
         @pl.when((role == 1) | (role == 3))
         def _():
             to_slot(slots.at[3, piece], 3, piece, 6, -1).wait_send()
-
-        @pl.when(((role == 3) & crosses(piece)) | ((role == 1) & crosses_back(piece)))
-        def _():
-            to_slot(slots.at[3, piece], 3, piece, 7, -3).wait_send()
 
         @pl.when(role == 2)
         def _():

time: 103 us -> 102 us (level)
  Pallas kernels: 98.4 us -> 97.2 us
    pallas_call x1, Pallas kernels: 98.4 us -> 97.2 us  [shards(): pl.pallas_call(functools.partial(block_kernel, n), out_shape=(jax.ShapeDt...]
where the time goes in v9:
time: 102 us
  Pallas kernels  97.2 us (95%)
  local copies, waits for them, and re-layouts  3.15 us (3%)
  between operations  1.3 us (1%)
    pallas_call x1, Pallas kernels, shards(): pl.pallas_call(functools.partial(block_kernel, n), out_shape=(jax.ShapeDt...  97.2 us
    unnamed x4, local copies, waits for them, and re-layouts  3.15 us

profile of v9, /device:TPU:0, one launch (start us, length us, event | category | flops | bytes accessed | tf_op | source)
XLA Modules:
  0.0 101.7 jit_solution(2813290057583284436)
XLA Ops:
  1.3 97.2 %spans_and_decoder.1 = (bf16[256,2560]{1,0:T(8,128)(2,1)}, bf16[3,1,52,384]{3,2,1,0:T(8,128)(2,1)}) custom-call(s32[1]{0:T(128)S(6)} %copy.14.owner_ref, s32[3,16]{1,0:T(4,128)} %bitcast.3, s32[16]{0:T(128)} %lengths_ref.1, bf16[256,2560]{1,0:T(8,128)(2,1)} %q_ref.1, bf16[2,256,2560]{2,1,0:T(8,128)(2,1)} %kv_ref.1, bf16[3,1,52,384]{3,2,1,0:T(8,128)(2,1)} %frames_ref.1, ...), custom_call_target="tpu_custom_call" | custom-call | flops 4597612544 | bytes 13205504 | tf_op jit(solution)/shard_map/spans_and_decoder/pallas_call | solution.py:477
  98.5 0.0 copy-start
  98.5 2.5 %copy.15 = bf16[256,2560]{1,0:T(8,128)(2,1)} copy(bf16[256,2560]{1,0:T(8,128)(2,1)} %get-tuple-element.4) | data formatting | bytes 2621440
  101.0 0.0 copy-done
  101.0 0.7 copy.16
Async XLA Ops:
  98.5 2.5 %copy-start = (bf16[3,1,52,384]{3,2,1,0:T(8,128)(2,1)S(1)}, bf16[3,1,52,384]{3,2,1,0:T(8,128)(2,1)}, u32[]{:S(2)}) copy-start(bf16[3,1,52,384]{3,2,1,0:T(8,128)(2,1)} %get-tuple-element.5) | copy-start | bytes 359428
